TPU v7x, 32 devices: a whole 2x2x4 slice. The times are simulated.
32 devices in a mesh: row: 8 (over z, x), col: 4 (over y, core).
Axes of the slice: x: 2, y: 2, z: 4, core: 2. Of those that a mesh axis runs over, the one named last changes fastest.
Arguments:
- trailing: bfloat16 [16384, 2048], P('row', 'col'), may hold values from -6 to 6
- panel: float32 [16384, 256], P(('row', 'col')), may hold values from -1 to 1
- diag_inverse: float32 [256, 256], P(None, 'col'), may hold values from -1 to 2, as said below
Outputs:
- updated: bfloat16 [16384, 2048], P('row', 'col')
Inputs may be any that keep to these rules, and one draw needn't show every extreme that they name: `diag_inverse`: lower triangular with a positive diagonal.
All inputs are finite; a program needn't handle non-finite values.
Results may differ from a plain program's by a relative error of at most 0.0051.
Values may be sent and summed in bfloat16 or wider, within the bound.
No kernel may reach another device: no remote copies, remote signals or barrier semaphores. Data moves between devices by JAX's collectives and lax.ppermute only.
A program may use at most 64 MiB of HBM per device.

v0:
```python
import jax
import jax.numpy as jnp
from jax import lax
from jax.sharding import PartitionSpec as P

NB = 256
SBLK = 2


def from_root(value, axis, source):
    kept = jnp.where(lax.axis_index(axis) == source, value, 0).astype(value.dtype)
    return lax.psum(kept, axis)


def solve_rows(rows_in, inverse):
    return lax.dot_general(
        rows_in,
        inverse,
        (((1,), (1,)), ((), ())),
        precision=lax.Precision.HIGHEST,
        preferred_element_type=jnp.float32,
    ).astype(jnp.bfloat16)


def local(trailing, panel, diag_inverse):
    inverse = lax.all_gather(diag_inverse, "col", axis=1, tiled=True)
    raw_rows = lax.all_gather(panel, "col", axis=0, tiled=True)
    solved = solve_rows(raw_rows, inverse)
    top_block = solved[:NB]
    col_index = lax.axis_index("col")
    col_count = lax.axis_size("col")
    pieces = []
    for section in range(SBLK):
        pieces.append(from_root(top_block, "row", col_index + section * col_count))
    mirror = jnp.concatenate(pieces, 0)
    update = lax.dot_general(
        solved, mirror, (((1,), (1,)), ((), ())), preferred_element_type=jnp.float32
    )
    return (trailing.astype(jnp.float32) - update).astype(jnp.bfloat16)


def solution(mesh):
    in_specs = (P("row", "col"), P(("row", "col"), None), P(None, "col"))
    out_specs = P("row", "col")
    return jax.shard_map(local, mesh=mesh, in_specs=in_specs, out_specs=out_specs, check_vma=False)
```

profile of v0, /device:TPU:0, one launch (start us, length us, event | category | flops | bytes accessed | tf_op | source)
XLA Modules:
  0.0 119.3 jit_solution(2830768427787437074)
XLA Ops:
  6.5 0.0 all-gather.2.cloned.1.call-start
  6.5 0.7 all-gather.2.cloned.1.call-update
  7.3 0.0 all-reduce.3.cloned.1.call-start
  7.3 7.4 %all_gather.7 = f32[256,256]{0,1:T(8,128)S(1)} all-gather(f32[256,64]{0,1:T(8,128)} %param.5), channel_id=1, replica_groups=mesh['row'=8,'col'=4] {'col'}, dimensions={1}, use_global_device_ids=true | all-gather | bytes 327680 | tf_op jit(solution)/shard_map/all_gather | solution.py:26
  14.7 0.0 copy-start
  14.7 19.5 %all-gather.2.cloned.1.call-done = f32[2048,256]{1,0:T(8,128)} async-done(((f32[512,256]{1,0:T(8,128)}), f32[2048,256]{1,0:T(8,128)}) %all-gather.2.cloned.1.call-update) | async-done | bytes 2097168 | tf_op jit(solution)/shard_map/all_gather | solution.py:27
  34.2 3.4 %convolution_convert_fusion = bf16[2048,256]{1,0:T(8,128)(2,1)S(1)} fusion(f32[2048,256]{1,0:T(8,128)} %all-gather.2.cloned.1.call-done, f32[256,256]{0,1:T(8,128)S(1)} %all_gather.7), kind=kOutput, calls=%fused_computation.1 | convolution fusion | flops 1611137024 | bytes 3407872 | tf_op jit(solution)/shard_map/dot_general | solution.py:16
  37.6 0.7 broadcast_select_fusion.1
  38.4 0.0 all-reduce.3.cloned.1.call-update
  38.4 71.0 %all-reduce.3.cloned.1.call-done = (bf16[256,256]{1,0:T(8,128)(2,1)}, bf16[256,256]{1,0:T(8,128)(2,1)}) async-done(((bf16[256,256]{1,0:T(8,128)(2,1)}, bf16[256,256]{1,0:T(8,128)(2,1)}), (bf16[256,256]{1,0:T(8,128)(2,1)}, bf16[256,256]{1,0:T(8,128)(2,1)})) %all-reduce.3.cloned.1.call-update) | async-done | bytes 262160 | tf_op jit(solution)/shard_map/psum | solution.py:12
  109.4 0.0 copy-done
  109.4 3.0 %subtract_convert_fusion = bf16[2048,512]{1,0:T(8,128)(2,1)} fusion(bf16[2048,512]{1,0:T(8,128)(2,1)S(1)} %copy-done, bf16[2048,256]{1,0:T(8,128)(2,1)S(1)} %convolution_convert_fusion, bf16[256,256]{1,0:T(8,128)(2,1)} %get-tuple-element.5, bf16[256,256]{1,0:T(8,128)(2,1)} %get-tuple-element.6), kind=kOutput, calls=%fused_computation | convolution fusion | flops 540540928 | bytes 5505024 | tf_op jit(solution)/shard_map/dot_general | solution.py:36
Async XLA Ops:
  6.5 27.7 %all-gather.2.cloned.1.call-start = ((), (), s32[]{:S(2)}) async-start(), calls=%async_computation | async-start | bytes 2621440 | tf_op jit(solution)/shard_map/all_gather | solution.py:27
  7.3 102.1 %all-reduce.3.cloned.1.call-start = ((), (), s32[]{:S(2)}) async-start(), calls=%async_computation.1 | async-start | bytes 524288 | tf_op jit(solution)/shard_map/psum | solution.py:12
  14.7 94.7 %copy-start = (bf16[2048,512]{1,0:T(8,128)(2,1)S(1)}, bf16[2048,512]{1,0:T(8,128)(2,1)}, u32[]{:S(2)}) copy-start(bf16[2048,512]{1,0:T(8,128)(2,1)} %param.3) | copy-start | bytes 6291460
Sparse Core Ops, SparseCore 0:
  8.9 25.2 all-gather.1
  38.5 70.8 all-reduce.2
where the time goes:
time: 119 us
  waiting for transfers between devices  91.2 us (77%)
  between operations  13.4 us (11%)
  blocking collectives  7.43 us (6%)
  matrix products  6.42 us (5%)
    psum x1, waiting for transfers between devices, from_root(): return lax.psum(kept, axis)  71 us
    all_gather x1, waiting for transfers between devices, local(): raw_rows = lax.all_gather(panel, 'col', axis=0, tiled=True)  19.5 us
    all_gather x1, blocking collectives, local(): inverse = lax.all_gather(diag_inverse, 'col', axis=1, tiled=True)  7.43 us
    dot_general x1, matrix products, solve_rows(): lax.dot_general(rows_in, inverse, (((1,), (1,)), ((), ())), precision=lax...  3.39 us
    dot_general x1, matrix products, local(): lax.dot_general(solved, mirror, (((1,), (1,)), ((), ())), preferred_eleme...  3.03 us
  transfers between devices with their start and end apart: 2, of which 2 were waited for; matrix products, arithmetic and copies ran while one was open for 0% of the time, Pallas kernels for 0%

commit v1 on v0

v1 whole, which is shorter than its diff:
```python
import jax
import jax.numpy as jnp
from jax import lax
from jax.experimental import pallas as pl
from jax.experimental.pallas import tpu as pltpu
from jax.sharding import PartitionSpec as P

NB = 256
SBLK = 2
SCALE = 32768.0
AXES = ("row", "col")
F32, F16, BF16 = jnp.float32, jnp.float16, jnp.bfloat16


def from_root(value, axis, source):
    kept = jnp.where(lax.axis_index(axis) == source, value, 0).astype(value.dtype)
    return lax.psum(kept, axis)


def solve_rows(rows_in, inverse):
    return lax.dot_general(
        rows_in,
        inverse,
        (((1,), (1,)), ((), ())),
        precision=lax.Precision.HIGHEST,
        preferred_element_type=F32,
    ).astype(BF16)


def local_any(trailing, panel, diag_inverse):
    inverse = lax.all_gather(diag_inverse, "col", axis=1, tiled=True)
    raw_rows = lax.all_gather(panel, "col", axis=0, tiled=True)
    solved = solve_rows(raw_rows, inverse)
    top_block = solved[:NB]
    col_index = lax.axis_index("col")
    col_count = lax.axis_size("col")
    pieces = []
    for section in range(SBLK):
        pieces.append(from_root(top_block, "row", col_index + section * col_count))
    mirror = jnp.concatenate(pieces, 0)
    update = lax.dot_general(
        solved, mirror, (((1,), (1,)), ((), ())), preferred_element_type=F32
    )
    return (trailing.astype(F32) - update).astype(BF16)


def dev(z, x, y, k):
    return (z * 2 + x) * 4 + y * 2 + k


ALL = [(z, x, y, k) for z in range(4) for x in range(2) for y in range(2) for k in range(2)]
CORE = [(dev(z, x, y, k), dev(z, x, y, 1 - k)) for z, x, y, k in ALL]
ACROSS = [(dev(z, x, y, k), dev(z, x, 1 - y, k)) for z, x, y, k in ALL]


def spread(j):
    pairs = []
    for z in range(4):
        for x in range(2):
            pairs.append((dev(z, x, 0, 1 - x), dev(z ^ j, x, z % 2, x)))
            for y in range(2):
                pairs.append((dev(z, x, y, x), dev(z, x, y, 1 - x)))
            back = 0 if (z ^ j) % 2 == 1 else 1
            pairs.append((dev(z, x, 1, 1 - x), dev(z, x, back, x)))
    return pairs


ASIDE = [
    (dev(z, x, y, k), dev(z, 1 - x, y, k) if k == x else dev(z, x, y, 1 - k))
    for z, x, y, k in ALL
]


def send(value, pairs):
    return lax.ppermute(value, AXES, pairs)


def split(value):
    high = value.astype(BF16)
    return high, (value - high.astype(F32)).astype(BF16)


def mul(a, b):
    return jnp.dot(a, b, preferred_element_type=F32)


def solve(rows, lt_hi, lt_lo):
    hi, lo = split(rows)
    return (mul(hi, lt_hi) + (mul(hi, lt_lo) + mul(lo, lt_hi))).astype(BF16)


def early_kernel(c_ref, own_ref, mate_ref, l0, l1, l2, l3, s_ref, hi_ref, lo_ref, lt_ref):
    c = c_ref[0]
    for i, block in enumerate((l0, l1, l2, l3)):
        at = pl.multiple_of((c ^ i) * 64, 64)
        lt_ref[pl.ds(at, 64), :] = block[...]
    hi, lo = split(lt_ref[...])
    hi_ref[...] = hi
    lo_ref[...] = lo
    s_ref[0] = solve(own_ref[...], hi, lo)
    s_ref[1] = solve(mate_ref[...], hi, lo)


def early(c, own, mate, blocks):
    vmem = pl.BlockSpec(memory_space=pltpu.VMEM)
    n = own.shape[0]
    return pl.pallas_call(
        early_kernel,
        out_shape=(
            jax.ShapeDtypeStruct((2, n, NB), BF16),
            jax.ShapeDtypeStruct((NB, NB), BF16),
            jax.ShapeDtypeStruct((NB, NB), BF16),
        ),
        in_specs=[pl.BlockSpec(memory_space=pltpu.SMEM)] + [vmem] * 6,
        out_specs=(vmem, vmem, vmem),
        scratch_shapes=[pltpu.VMEM((NB, NB), F32)],
        compiler_params=pltpu.CompilerParams(vmem_limit_bytes=24 * 1024 * 1024),
    )(c, own, mate, *blocks)


def final_kernel(c_ref, t_ref, s_ref, y0, y1, ky0, ky1, ta, tb, hi_ref, lo_ref, o_ref, m_ref, w_ref):
    i = pl.program_id(0)
    half = y0.shape[0]

    @pl.when(i == 0)
    def _():
        hi, lo = hi_ref[...], lo_ref[...]
        m_ref[:NB] = solve(ta[...], hi, lo)
        m_ref[NB:] = solve(tb[...], hi, lo)

    @pl.when(i < 2)
    def _():
        w_ref[...] = s_ref[i]

    @pl.when(i == 2)
    def _():
        hi, lo = hi_ref[...], lo_ref[...]
        w_ref[:half] = solve(y0[...], hi, lo)
        w_ref[half:] = solve(y1[...], hi, lo)

    @pl.when(i == 3)
    def _():
        hi, lo = hi_ref[...], lo_ref[...]
        w_ref[:half] = solve(ky0[...], hi, lo)
        w_ref[half:] = solve(ky1[...], hi, lo)

    update = lax.dot_general(
        w_ref[...], m_ref[...], (((1,), (1,)), ((), ())), preferred_element_type=F32
    )
    o_ref[...] = (t_ref[...].astype(F32) - update).astype(BF16)


def final(c, trailing, s, rest, ta, tb, hi, lo):
    rows, cols = trailing.shape
    n = rows // 4
    vmem = pl.BlockSpec(memory_space=pltpu.VMEM)
    block = pl.BlockSpec((n, cols), lambda i, c_ref: (c_ref[0] ^ i, 0))
    return pl.pallas_call(
        final_kernel,
        out_shape=jax.ShapeDtypeStruct((rows, cols), BF16),
        grid_spec=pltpu.PrefetchScalarGridSpec(
            num_scalar_prefetch=1,
            grid=(4,),
            in_specs=[block] + [vmem] * 9,
            out_specs=block,
            scratch_shapes=[
                pltpu.VMEM((2 * NB, NB), BF16),
                pltpu.VMEM((n, NB), BF16),
            ],
        ),
        compiler_params=pltpu.CompilerParams(vmem_limit_bytes=24 * 1024 * 1024),
    )(c, trailing, s, *rest, ta, tb, hi, lo)


def widen(value):
    return value.astype(F32) * (1.0 / SCALE)


def local_8x4(trailing, panel, diag_inverse):
    row, col = lax.axis_index("row"), lax.axis_index("col")
    z, x, y, k = row // 2, row % 2, col // 2, col % 2
    barrier = lax.optimization_barrier
    c = jnp.full((1,), col, jnp.int32)
    inv = diag_inverse.T
    n = panel.shape[0]

    mate = send(panel, CORE)
    inv_y = send(inv, ACROSS)
    p0 = (panel[:NB] * SCALE).astype(F16)
    p1 = (panel[NB:] * SCALE).astype(F16)
    y0 = send(p0, ACROSS)
    top = (jnp.where(k == 0, panel[:NB], mate[:NB]) * SCALE).astype(F16)
    r1, r2, r3 = (send(top, spread(j)) for j in (1, 2, 3))
    y1 = send(p1, ACROSS)
    y0, r1 = barrier((y0, r1))
    ky0 = send(y0, CORE)
    across_top = jnp.where(k == 0, y0, ky0)
    same = z % 2 == y
    q0 = jnp.where(same, jnp.where(y == 0, top, across_top), r1)
    q1 = jnp.where(same, r2, r3)
    x0, x1 = send(q0, ASIDE), send(q1, ASIDE)
    inv_k = send(inv, CORE)
    inv_ky = send(inv_y, CORE)
    s, hi, lo = early(c, panel, mate, (inv, inv_k, inv_y, inv_ky))
    ky1 = send(y1, CORE)
    here = x == k
    a = jnp.where(here, q0, x0)
    b = jnp.where(here, q1, x1)
    ta = widen(jnp.where(z < 2, a, b))
    tb = widen(jnp.where(z < 2, b, a))
    rest = [widen(v) for v in (y0, y1, ky0, ky1)]
    return final(c, trailing, s, rest, ta, tb, hi, lo)


def solution(mesh):
    in_specs = (P("row", "col"), P(("row", "col"), None), P(None, "col"))
    out_specs = P("row", "col")
    fits = mesh.shape["row"] == 8 and mesh.shape["col"] == 4
    return jax.shard_map(
        local_8x4 if fits else local_any,
        mesh=mesh,
        in_specs=in_specs,
        out_specs=out_specs,
        check_vma=False,
    )
```

time: 119 us -> 28.9 us (0.24)
  waiting for transfers between devices: 91.2 us -> 6.89 us
  starting transfers between devices: 0.04 us -> 13.9 us
  between operations: 13.4 us -> 0.11 us
  blocking collectives: 7.43 us -> 0 us
  matrix products: 6.42 us -> 0 us
  Pallas kernels: 0 us -> 4.44 us
  local copies, waits for them, and re-layouts: 0.01 us -> 1.89 us
    psum x1 -> x0, waiting for transfers between devices: 71 us -> none  [from_root(): return lax.psum(kept, axis)]
    all_gather x1 -> x0, waiting for transfers between devices: 19.5 us -> none  [local(): raw_rows = lax.all_gather(panel, 'col', axis=0, tiled=True)]
    ppermute x0 -> x13, starting transfers between devices: none -> 13.9 us  [send(): return lax.ppermute(value, AXES, pairs)]
    all_gather x1 -> x0, blocking collectives: 7.43 us -> none  [local(): inverse = lax.all_gather(diag_inverse, 'col', axis=1, tiled=True)]
    ppermute x0 -> x13, waiting for transfers between devices: none -> 6.89 us  [send(): return lax.ppermute(value, AXES, pairs)]
    dot_general x2 -> x0, matrix products: 6.42 us -> none  [the longest x1 3.39 us: solve_rows(): lax.dot_general(rows_in, inverse, (((1,), (1,)), ((), ())), precision=lax...]
    pallas_call x0 -> x2, Pallas kernels: none -> 4.44 us  [the longest x1 3.83 us: final(): pl.pallas_call(final_kernel, out_shape=jax.ShapeDtypeStruct((rows, cols),...]
    unnamed x2 -> x6, local copies, waits for them, and re-layouts: 0.01 us -> 1.89 us
  transfers between devices with their start and end apart: 2 -> 13, of which waited for: 2 -> 4; matrix products, arithmetic and copies ran while one was open for 0% -> 5% of each run, Pallas kernels for 0% -> 2%
where the time goes in v1:
time: 28.9 us; the launch traced here: 28.7 us
  starting transfers between devices  13.9 us (48%)
  waiting for transfers between devices  6.89 us (24%)
  Pallas kernels  4.44 us (15%)
  local copies, waits for them, and re-layouts  1.89 us (7%)
  other arithmetic  1.44 us (5%)
    ppermute x13, starting transfers between devices, send(): return lax.ppermute(value, AXES, pairs)  13.9 us
    ppermute x13, waiting for transfers between devices, send(): return lax.ppermute(value, AXES, pairs)  6.89 us
    pallas_call x1, Pallas kernels, final(): pl.pallas_call(final_kernel, out_shape=jax.ShapeDtypeStruct((rows, cols),...  3.83 us
    unnamed x6, local copies, waits for them, and re-layouts  1.89 us
    convert_element_type x1, other arithmetic, local_8x4(): p1 = (panel[NB:] * SCALE).astype(F16)  1.12 us
    pallas_call x1, Pallas kernels, early(): pl.pallas_call(early_kernel, out_shape=(jax.ShapeDtypeStruct((2, n, NB),...  0.61 us
  transfers between devices with their start and end apart: 13, of which 4 were waited for; matrix products, arithmetic and copies ran while one was open for 5% of the time, Pallas kernels for 2%

profile of v1, /device:TPU:0, one launch (start us, length us, event | category | flops | bytes accessed | tf_op | source)
XLA Modules:
  0.0 28.7 jit_solution(17224397962194093210)
XLA Ops:
  0.0 0.5 %collective-permute-start = (f32[512,256]{1,0:T(8,128)}, f32[512,256]{1,0:T(8,128)S(1)}, u32[]{:S(2)}, u32[]{:S(2)}) collective-permute-start(f32[512,256]{1,0:T(8,128)} %own_ref.1), channel_id=1, source_target_pairs={{0,1},{1,0},{2,3},{3,2},{4,5},{5,4},{6,7},{7,6},{8,9},{9,8},{10,11... | collective-permute-start | bytes 1572872 | tf_op jit(solution)/shard_map/ppermute | solution.py:75
  0.5 2.5 %collective-permute-start.2 = (f32[64,256]{1,0:T(8,128)}, f32[64,256]{1,0:T(8,128)S(1)}, u32[]{:S(2)}, u32[]{:S(2)}) collective-permute-start(f32[64,256]{1,0:T(8,128)} %bitcast.2), channel_id=1, source_target_pairs={{0,2},{1,3},{2,0},{3,1},{4,6},{5,7},{6,4},{7,5},{8,10},{9,11},{10,... | collective-permute-start | bytes 196616 | tf_op jit(solution)/shard_map/ppermute | solution.py:75
  3.0 1.1 %multiply_convert_fusion = (f16[256,256]{1,0:T(8,128)(2,1)S(1)}, f16[256,256]{1,0:T(8,128)(2,1)S(1)}, f16[256,256]{1,0:T(8,128)(2,1)S(1)}) fusion(f32[512,256]{1,0:T(8,128)} %own_ref.1, f32[512,256]{1,0:T(8,128)S(1)} %collective-permute-done.mate_ref, pred[]{:T(512)S(6)} %eq.17), kind=kLoop, calls=%fused_computation.8 | loop fusion | flops 458752 | bytes 1179649 | tf_op jit(solution)/shard_map/convert_element_type | solution.py:190
  4.1 0.3 collective-permute-start.11
  4.4 4.1 %collective-permute-start.10 = (f16[256,256]{1,0:T(8,128)(2,1)S(1)}, f16[256,256]{1,0:T(8,128)(2,1)S(1)}, u32[]{:S(2)}, u32[]{:S(2)}) collective-permute-start(f16[256,256]{1,0:T(8,128)(2,1)S(1)} %get-tuple-element.18), channel_id=1, source_target_pairs={{1,16},{0,1},{2,3},{3,2},{4,21},{5,4},{7,6},{6,7},{9,26},{8,9},{10... | collective-permute-start | bytes 393224 | tf_op jit(solution)/shard_map/ppermute | solution.py:75
  8.5 0.0 collective-permute-start.1
  8.5 0.0 collective-permute-done.2.l2
  8.5 0.5 %collective-permute-start.3 = (f32[64,256]{1,0:T(8,128)S(1)}, f32[64,256]{1,0:T(8,128)S(1)}, u32[]{:S(2)}, u32[]{:S(2)}) collective-permute-start(f32[64,256]{1,0:T(8,128)S(1)} %collective-permute-done.2.l2), channel_id=1, source_target_pairs={{0,1},{1,0},{2,3},{3,2},{4,5},{5,4},{6,7},{7,6},{8,9},{9,8},{10,11... | collective-permute-start | bytes 196616 | tf_op jit(solution)/shard_map/ppermute | solution.py:75
  9.0 0.0 collective-permute-start.5
  9.0 1.0 %collective-permute-done.1.l1 = f32[64,256]{1,0:T(8,128)S(1)} collective-permute-done((f32[64,256]{1,0:T(8,128)}, f32[64,256]{1,0:T(8,128)S(1)}, u32[]{:S(2)}, u32[]{:S(2)}) %collective-permute-start.1) | collective-permute-done | bytes 65568 | tf_op jit(solution)/shard_map/ppermute | solution.py:75
  9.9 0.0 collective-permute-start.6
  10.0 0.0 collective-permute-done.3.l3
  10.0 2.0 %collective-permute-start.4 = (f16[256,256]{1,0:T(8,128)(2,1)S(1)}, f16[256,256]{1,0:T(8,128)(2,1)S(1)}, u32[]{:S(2)}, u32[]{:S(2)}) collective-permute-start(f16[256,256]{1,0:T(8,128)(2,1)S(1)} %get-tuple-element.19), channel_id=1, source_target_pairs={{0,2},{1,3},{2,0},{3,1},{4,6},{5,7},{6,4},{7,5},{8,10},{9,11},{10,... | collective-permute-start | bytes 393224 | tf_op jit(solution)/shard_map/ppermute | solution.py:75
  12.0 1.0 %copy-done = f32[512,256]{1,0:T(8,128)S(1)} copy-done((f32[512,256]{1,0:T(8,128)S(1)}, f32[512,256]{1,0:T(8,128)}, u32[]{:S(2)}) %copy-start) | copy-done | bytes 524312
  13.0 0.8 %copy-done.2 = f32[256,64]{0,1:T(8,128)S(1)} copy-done((f32[256,64]{0,1:T(8,128)S(1)}, f32[256,64]{0,1:T(8,128)}, u32[]{:S(2)}) %copy-start.2) | copy-done | bytes 65560
  13.9 0.6 %shard_map.37 = (bf16[2,512,256]{2,1,0:T(8,128)(2,1)S(1)}, bf16[256,256]{1,0:T(8,128)(2,1)S(1)}, bf16[256,256]{1,0:T(8,128)(2,1)S(1)}) custom-call(s32[1]{0:T(128)} %bitcast.c_ref, f32[512,256]{1,0:T(8,128)S(1)} %copy-done, f32[512,256]{1,0:T(8,128)S(1)} %collective-permute-done.mate_ref, f32[64,256]{1,0:T(8,128)S(1)} %bitcast.4, ...), custom_call_target="tpu_custom_call" | custom-call | tf_op jit(solution)/shard_map/pallas_call | solution.py:107
  14.5 0.0 copy-start.1
  14.5 0.0 collective-permute-done.11
  14.5 0.0 collective-permute-done.10
  14.6 1.7 %collective-permute-start.12 = (f16[256,256]{1,0:T(8,128)(2,1)S(1)}, f16[256,256]{1,0:T(8,128)(2,1)S(1)}, u32[]{:S(2)}, u32[]{:S(2)}) collective-permute-start(f16[256,256]{1,0:T(8,128)(2,1)S(1)} %broadcast_select_fusion), channel_id=1, source_target_pairs={{0,4},{1,0},{2,6},{3,2},{4,5},{5,1},{6,7},{7,3},{8,12},{9,8},{10,1... | collective-permute-start | bytes 393224 | tf_op jit(solution)/shard_map/ppermute | solution.py:75
  16.2 2.8 %collective-permute-done.4 = f16[256,256]{1,0:T(8,128)(2,1)S(1)} collective-permute-done((f16[256,256]{1,0:T(8,128)(2,1)S(1)}, f16[256,256]{1,0:T(8,128)(2,1)S(1)}, u32[]{:S(2)}, u32[]{:S(2)}) %collective-permute-start.4) | collective-permute-done | bytes 131104 | tf_op jit(solution)/shard_map/ppermute | solution.py:75
  19.0 0.0 collective-permute-done.5
  19.0 0.0 collective-permute-start.7
  19.0 0.0 collective-permute-done.6
  19.0 0.6 %collective-permute-start.8 = (f16[256,256]{1,0:T(8,128)(2,1)S(1)}, f16[256,256]{1,0:T(8,128)(2,1)S(1)}, u32[]{:S(2)}, u32[]{:S(2)}) collective-permute-start(f16[256,256]{1,0:T(8,128)(2,1)S(1)} %collective-permute-done.6), channel_id=1, source_target_pairs={{0,1},{1,0},{2,3},{3,2},{4,5},{5,4},{6,7},{7,6},{8,9},{9,8},{10,11... | collective-permute-start | bytes 393224 | tf_op jit(solution)/shard_map/ppermute | solution.py:75
  19.6 0.7 %collective-permute-done.7 = f16[256,256]{1,0:T(8,128)(2,1)S(1)} collective-permute-done((f16[256,256]{1,0:T(8,128)(2,1)S(1)}, f16[256,256]{1,0:T(8,128)(2,1)S(1)}, u32[]{:S(2)}, u32[]{:S(2)}) %collective-permute-start.7) | collective-permute-done | bytes 131104 | tf_op jit(solution)/shard_map/ppermute | solution.py:75
  20.3 0.1 select_select_fusion
  20.4 1.8 %collective-permute-start.9 = (f16[256,256]{1,0:T(8,128)(2,1)S(1)}, f16[256,256]{1,0:T(8,128)(2,1)S(1)}, u32[]{:S(2)}, u32[]{:S(2)}) collective-permute-start(f16[256,256]{1,0:T(8,128)(2,1)S(1)} %select_select_fusion), channel_id=1, source_target_pairs={{0,4},{1,0},{2,6},{3,2},{4,5},{5,1},{6,7},{7,3},{8,12},{9,8},{10,1... | collective-permute-start | bytes 393224 | tf_op jit(solution)/shard_map/ppermute | solution.py:75
  22.3 0.0 collective-permute-done.12
  22.3 2.4 %collective-permute-done.9 = f16[256,256]{1,0:T(8,128)(2,1)S(1)} collective-permute-done((f16[256,256]{1,0:T(8,128)(2,1)S(1)}, f16[256,256]{1,0:T(8,128)(2,1)S(1)}, u32[]{:S(2)}, u32[]{:S(2)}) %collective-permute-start.9) | collective-permute-done | bytes 131104 | tf_op jit(solution)/shard_map/ppermute | solution.py:75
  24.8 0.1 convert_multiply_fusion
  24.9 3.8 %shard_map.38 = bf16[2048,512]{1,0:T(8,128)(2,1)} custom-call(s32[1]{0:T(128)} %bitcast.c_ref, bf16[2048,512]{1,0:T(8,128)(2,1)S(1)} %copy-done.1, bf16[2,512,256]{2,1,0:T(8,128)(2,1)S(1)} %get-tuple-element.10.s_ref, f32[256,256]{1,0:T(8,128)S(1)} %convert_multiply_fusion.5.y0, f32[256,256]{1,0:T(8,128)S(1)} %convert_multiply_fusion.4.y1, ...), custom_call_target="tpu_custom_call" | custom-call | tf_op jit(solution)/shard_map/pallas_call | solution.py:158
  (10 shorter events, 0.2 us)
Async XLA Ops:
  0.0 3.0 %collective-permute-start = (f32[512,256]{1,0:T(8,128)}, f32[512,256]{1,0:T(8,128)S(1)}, u32[]{:S(2)}, u32[]{:S(2)}) collective-permute-start(f32[512,256]{1,0:T(8,128)} %own_ref.1), channel_id=1, source_target_pairs={{0,1},{1,0},{2,3},{3,2},{4,5},{5,4},{6,7},{7,6},{8,9},{9,8},{10,11... | collective-permute-start | bytes 1572872 | tf_op jit(solution)/shard_map/ppermute | solution.py:75
  0.5 8.0 %collective-permute-start.2 = (f32[64,256]{1,0:T(8,128)}, f32[64,256]{1,0:T(8,128)S(1)}, u32[]{:S(2)}, u32[]{:S(2)}) collective-permute-start(f32[64,256]{1,0:T(8,128)} %bitcast.2), channel_id=1, source_target_pairs={{0,2},{1,3},{2,0},{3,1},{4,6},{5,7},{6,4},{7,5},{8,10},{9,11},{10,... | collective-permute-start | bytes 196616 | tf_op jit(solution)/shard_map/ppermute | solution.py:75
  4.1 10.4 %collective-permute-start.11 = (f16[256,256]{1,0:T(8,128)(2,1)S(1)}, f16[256,256]{1,0:T(8,128)(2,1)S(1)}, u32[]{:S(2)}, u32[]{:S(2)}) collective-permute-start(f16[256,256]{1,0:T(8,128)(2,1)S(1)} %get-tuple-element.18), channel_id=1, source_target_pairs={{1,24},{0,1},{2,3},{3,0},{4,29},{5,4},{7,6},{6,5},{9,18},{8,9},{10... | collective-permute-start | bytes 393224 | tf_op jit(solution)/shard_map/ppermute | solution.py:75
  4.4 10.1 %collective-permute-start.10 = (f16[256,256]{1,0:T(8,128)(2,1)S(1)}, f16[256,256]{1,0:T(8,128)(2,1)S(1)}, u32[]{:S(2)}, u32[]{:S(2)}) collective-permute-start(f16[256,256]{1,0:T(8,128)(2,1)S(1)} %get-tuple-element.18), channel_id=1, source_target_pairs={{1,16},{0,1},{2,3},{3,2},{4,21},{5,4},{7,6},{6,7},{9,26},{8,9},{10... | collective-permute-start | bytes 393224 | tf_op jit(solution)/shard_map/ppermute | solution.py:75
  8.5 1.5 %collective-permute-start.1 = (f32[64,256]{1,0:T(8,128)}, f32[64,256]{1,0:T(8,128)S(1)}, u32[]{:S(2)}, u32[]{:S(2)}) collective-permute-start(f32[64,256]{1,0:T(8,128)} %bitcast.3), channel_id=1, source_target_pairs={{0,1},{1,0},{2,3},{3,2},{4,5},{5,4},{6,7},{7,6},{8,9},{9,8},{10,11... | collective-permute-start | bytes 196616 | tf_op jit(solution)/shard_map/ppermute | solution.py:75
  8.5 1.5 %collective-permute-start.3 = (f32[64,256]{1,0:T(8,128)S(1)}, f32[64,256]{1,0:T(8,128)S(1)}, u32[]{:S(2)}, u32[]{:S(2)}) collective-permute-start(f32[64,256]{1,0:T(8,128)S(1)} %collective-permute-done.2.l2), channel_id=1, source_target_pairs={{0,1},{1,0},{2,3},{3,2},{4,5},{5,4},{6,7},{7,6},{8,9},{9,8},{10,11... | collective-permute-start | bytes 196616 | tf_op jit(solution)/shard_map/ppermute | solution.py:75
  9.0 10.0 %collective-permute-start.5 = (f16[256,256]{1,0:T(8,128)(2,1)S(1)}, f16[256,256]{1,0:T(8,128)(2,1)S(1)}, u32[]{:S(2)}, u32[]{:S(2)}) collective-permute-start(f16[256,256]{1,0:T(8,128)(2,1)S(1)} %get-tuple-element.18), channel_id=1, source_target_pairs={{1,8},{0,1},{2,3},{3,0},{4,13},{5,4},{7,6},{6,5},{9,2},{8,9},{10,1... | collective-permute-start | bytes 393224 | tf_op jit(solution)/shard_map/ppermute | solution.py:75
  9.9 9.1 %collective-permute-start.6 = (f16[256,256]{1,0:T(8,128)(2,1)S(1)}, f16[256,256]{1,0:T(8,128)(2,1)S(1)}, u32[]{:S(2)}, u32[]{:S(2)}) collective-permute-start(f16[256,256]{1,0:T(8,128)(2,1)S(1)} %get-tuple-element.17), channel_id=1, source_target_pairs={{0,2},{1,3},{2,0},{3,1},{4,6},{5,7},{6,4},{7,5},{8,10},{9,11},{10,... | collective-permute-start | bytes 393224 | tf_op jit(solution)/shard_map/ppermute | solution.py:75
  10.0 9.0 %collective-permute-start.4 = (f16[256,256]{1,0:T(8,128)(2,1)S(1)}, f16[256,256]{1,0:T(8,128)(2,1)S(1)}, u32[]{:S(2)}, u32[]{:S(2)}) collective-permute-start(f16[256,256]{1,0:T(8,128)(2,1)S(1)} %get-tuple-element.19), channel_id=1, source_target_pairs={{0,2},{1,3},{2,0},{3,1},{4,6},{5,7},{6,4},{7,5},{8,10},{9,11},{10,... | collective-permute-start | bytes 393224 | tf_op jit(solution)/shard_map/ppermute | solution.py:75
  12.0 1.0 %copy-start = (f32[512,256]{1,0:T(8,128)S(1)}, f32[512,256]{1,0:T(8,128)}, u32[]{:S(2)}) copy-start(f32[512,256]{1,0:T(8,128)} %own_ref.1) | copy-start | bytes 1572868
  13.0 0.8 %copy-start.2 = (f32[256,64]{0,1:T(8,128)S(1)}, f32[256,64]{0,1:T(8,128)}, u32[]{:S(2)}) copy-start(f32[256,64]{0,1:T(8,128)} %param.5) | copy-start | bytes 196612
  14.5 10.4 %copy-start.1 = (bf16[2048,512]{1,0:T(8,128)(2,1)S(1)}, bf16[2048,512]{1,0:T(8,128)(2,1)}, u32[]{:S(2)}) copy-start(bf16[2048,512]{1,0:T(8,128)(2,1)} %t_ref.1) | copy-start | bytes 6291460
  14.6 7.8 %collective-permute-start.12 = (f16[256,256]{1,0:T(8,128)(2,1)S(1)}, f16[256,256]{1,0:T(8,128)(2,1)S(1)}, u32[]{:S(2)}, u32[]{:S(2)}) collective-permute-start(f16[256,256]{1,0:T(8,128)(2,1)S(1)} %broadcast_select_fusion), channel_id=1, source_target_pairs={{0,4},{1,0},{2,6},{3,2},{4,5},{5,1},{6,7},{7,3},{8,12},{9,8},{10,1... | collective-permute-start | bytes 393224 | tf_op jit(solution)/shard_map/ppermute | solution.py:75
  19.0 1.3 %collective-permute-start.7 = (f16[256,256]{1,0:T(8,128)(2,1)S(1)}, f16[256,256]{1,0:T(8,128)(2,1)S(1)}, u32[]{:S(2)}, u32[]{:S(2)}) collective-permute-start(f16[256,256]{1,0:T(8,128)(2,1)S(1)} %collective-permute-done.4), channel_id=1, source_target_pairs={{0,1},{1,0},{2,3},{3,2},{4,5},{5,4},{6,7},{7,6},{8,9},{9,8},{10,11... | collective-permute-start | bytes 393224 | tf_op jit(solution)/shard_map/ppermute | solution.py:75
  19.0 3.2 %collective-permute-start.8 = (f16[256,256]{1,0:T(8,128)(2,1)S(1)}, f16[256,256]{1,0:T(8,128)(2,1)S(1)}, u32[]{:S(2)}, u32[]{:S(2)}) collective-permute-start(f16[256,256]{1,0:T(8,128)(2,1)S(1)} %collective-permute-done.6), channel_id=1, source_target_pairs={{0,1},{1,0},{2,3},{3,2},{4,5},{5,4},{6,7},{7,6},{8,9},{9,8},{10,11... | collective-permute-start | bytes 393224 | tf_op jit(solution)/shard_map/ppermute | solution.py:75
  20.4 4.3 %collective-permute-start.9 = (f16[256,256]{1,0:T(8,128)(2,1)S(1)}, f16[256,256]{1,0:T(8,128)(2,1)S(1)}, u32[]{:S(2)}, u32[]{:S(2)}) collective-permute-start(f16[256,256]{1,0:T(8,128)(2,1)S(1)} %select_select_fusion), channel_id=1, source_target_pairs={{0,4},{1,0},{2,6},{3,2},{4,5},{5,1},{6,7},{7,3},{8,12},{9,8},{10,1... | collective-permute-start | bytes 393224 | tf_op jit(solution)/shard_map/ppermute | solution.py:75

commit v2 on v1

v2 whole, which is shorter than its diff:
```python
import jax
import jax.numpy as jnp
from jax import lax
from jax.experimental import pallas as pl
from jax.experimental.pallas import tpu as pltpu
from jax.sharding import PartitionSpec as P

NB = 256
SBLK = 2
SCALE = 32768.0
AXES = ("row", "col")
F32, F16, BF16 = jnp.float32, jnp.float16, jnp.bfloat16


def from_root(value, axis, source):
    kept = jnp.where(lax.axis_index(axis) == source, value, 0).astype(value.dtype)
    return lax.psum(kept, axis)


def solve_rows(rows_in, inverse):
    return lax.dot_general(
        rows_in,
        inverse,
        (((1,), (1,)), ((), ())),
        precision=lax.Precision.HIGHEST,
        preferred_element_type=F32,
    ).astype(BF16)


def local_any(trailing, panel, diag_inverse):
    inverse = lax.all_gather(diag_inverse, "col", axis=1, tiled=True)
    raw_rows = lax.all_gather(panel, "col", axis=0, tiled=True)
    solved = solve_rows(raw_rows, inverse)
    top_block = solved[:NB]
    col_index = lax.axis_index("col")
    col_count = lax.axis_size("col")
    pieces = []
    for section in range(SBLK):
        pieces.append(from_root(top_block, "row", col_index + section * col_count))
    mirror = jnp.concatenate(pieces, 0)
    update = lax.dot_general(
        solved, mirror, (((1,), (1,)), ((), ())), preferred_element_type=F32
    )
    return (trailing.astype(F32) - update).astype(BF16)


def dev(z, x, y, k):
    return (z * 2 + x) * 4 + y * 2 + k


ALL = [(z, x, y, k) for z in range(4) for x in range(2) for y in range(2) for k in range(2)]
CORE = [(dev(z, x, y, k), dev(z, x, y, 1 - k)) for z, x, y, k in ALL]
ACROSS = [(dev(z, x, y, k), dev(z, x, 1 - y, k)) for z, x, y, k in ALL]


def spread_a():
    pairs = []
    for z in range(4):
        for x in range(2):
            pairs.append((dev(z, x, 0, x), dev(z ^ 1, x, z % 2, x)))
            pairs.append((dev(z, x, 0, 1 - x), dev(z ^ 2, x, z % 2, x)))
            pairs.append((dev(z, x, 1, x), dev(z, x, 1, 1 - x)))
            pairs.append((dev(z, x, 1, 1 - x), dev(z, x, 0, 1 - x)))
    return pairs


def spread_b():
    pairs = []
    for z in range(4):
        for x in range(2):
            pairs.append((dev(z, x, 0, x), dev(z ^ 3, x, z % 2, x)))
            if z % 2:
                pairs.append((dev(z, x, 0, 1 - x), dev(z, x, 1, x)))
                pairs.append((dev(z, x, 1, x), dev(z, x, 1, 1 - x)))
                pairs.append((dev(z, x, 1, 1 - x), dev(z, x, 0, 1 - x)))
            else:
                pairs.append((dev(z, x, 0, 1 - x), dev(z, x, 0, x)))
                pairs.append((dev(z, x, 1, x), dev(z, x, 1, 1 - x)))
                pairs.append((dev(z, x, 1, 1 - x), dev(z, x, 0, 1 - x)))
    return pairs


ASIDE = [
    (dev(z, x, y, k), dev(z, 1 - x, y, k) if k == x else dev(z, x, y, 1 - k))
    for z, x, y, k in ALL
]


def send(value, pairs):
    return lax.ppermute(value, AXES, pairs)


def split(value):
    high = value.astype(BF16)
    return high, (value - high.astype(F32)).astype(BF16)


def mul(a, b):
    return jnp.dot(a, b, preferred_element_type=F32)


def solve(rows, lt_hi, lt_lo):
    hi, lo = split(rows)
    return (mul(hi, lt_hi) + (mul(hi, lt_lo) + mul(lo, lt_hi))).astype(BF16)


def early_kernel(c_ref, own_ref, mate_ref, l0, l1, l2, l3, s_ref, hi_ref, lo_ref, lt_ref):
    c = c_ref[0]
    for i, block in enumerate((l0, l1, l2, l3)):
        at = pl.multiple_of((c ^ i) * 64, 64)
        lt_ref[pl.ds(at, 64), :] = block[...]
    hi, lo = split(lt_ref[...])
    hi_ref[...] = hi
    lo_ref[...] = lo
    s_ref[0] = solve(own_ref[...], hi, lo)
    s_ref[1] = solve(mate_ref[...], hi, lo)


VMEM = pl.BlockSpec(memory_space=pltpu.VMEM)
SMEM = pl.BlockSpec(memory_space=pltpu.SMEM)
LIMIT = pltpu.CompilerParams(vmem_limit_bytes=24 * 1024 * 1024)


def early(c, own, mate, blocks):
    n = own.shape[0]
    return pl.pallas_call(
        early_kernel,
        out_shape=(
            jax.ShapeDtypeStruct((2, n, NB), BF16),
            jax.ShapeDtypeStruct((NB, NB), BF16),
            jax.ShapeDtypeStruct((NB, NB), BF16),
        ),
        in_specs=[SMEM] + [VMEM] * 6,
        out_specs=(VMEM, VMEM, VMEM),
        scratch_shapes=[pltpu.VMEM((NB, NB), F32)],
        compiler_params=LIMIT,
    )(c, own, mate, *blocks)


def late_kernel(y0, y1, ky0, ky1, hi_ref, lo_ref, s_ref):
    hi, lo = hi_ref[...], lo_ref[...]
    half = y0.shape[0]
    s_ref[0, :half] = solve(y0[...], hi, lo)
    s_ref[0, half:] = solve(y1[...], hi, lo)
    s_ref[1, :half] = solve(ky0[...], hi, lo)
    s_ref[1, half:] = solve(ky1[...], hi, lo)


def late(rest, hi, lo):
    return pl.pallas_call(
        late_kernel,
        out_shape=jax.ShapeDtypeStruct((2, 2 * rest[0].shape[0], NB), BF16),
        in_specs=[VMEM] * 6,
        out_specs=VMEM,
        compiler_params=LIMIT,
    )(*rest, hi, lo)


def final_kernel(c_ref, t_ref, sa, sb, ta, tb, hi_ref, lo_ref, o_ref, m_ref, buf, sems):
    c = c_ref[0]
    n = sa.shape[1]
    hi, lo = hi_ref[...], lo_ref[...]
    m_ref[:NB] = solve(ta[...], hi, lo)
    m_ref[NB:] = solve(tb[...], hi, lo)
    mirror = m_ref[...]
    copies = []
    for i in range(4):
        at = pl.multiple_of((c ^ i) * n, n)
        rows = (sa if i < 2 else sb)[i % 2]
        update = lax.dot_general(
            rows, mirror, (((1,), (1,)), ((), ())), preferred_element_type=F32
        )
        buf[i] = (t_ref[pl.ds(at, n), :].astype(F32) - update).astype(BF16)
        copy = pltpu.make_async_copy(buf.at[i], o_ref.at[pl.ds(at, n), :], sems.at[i])
        copy.start()
        copies.append(copy)
    for copy in copies:
        copy.wait()


def final(c, trailing, sa, sb, ta, tb, hi, lo):
    rows, cols = trailing.shape
    n = rows // 4
    return pl.pallas_call(
        final_kernel,
        out_shape=jax.ShapeDtypeStruct((rows, cols), BF16),
        in_specs=[SMEM] + [VMEM] * 7,
        out_specs=pl.BlockSpec(memory_space=pl.ANY),
        scratch_shapes=[
            pltpu.VMEM((2 * NB, NB), BF16),
            pltpu.VMEM((4, n, cols), BF16),
            pltpu.SemaphoreType.DMA((4,)),
        ],
        compiler_params=LIMIT,
    )(c, trailing, sa, sb, ta, tb, hi, lo)


def widen(value):
    return value.astype(F32) * (1.0 / SCALE)


def narrow(value):
    return (value * SCALE).astype(F16)


def local_8x4(trailing, panel, diag_inverse):
    row, col = lax.axis_index("row"), lax.axis_index("col")
    z, x, y, k = row // 2, row % 2, col // 2, col % 2
    barrier = lax.optimization_barrier
    c = jnp.full((1,), col, jnp.int32)
    inv = diag_inverse.T

    mate = send(panel, CORE)
    inv_y = send(inv, ACROSS)
    y0 = send(narrow(panel[:NB]), ACROSS)
    y1 = send(narrow(panel[NB:]), ACROSS)
    top = narrow(jnp.where(k == 0, panel[:NB], mate[:NB]))
    ra, rb = send(top, spread_a()), send(top, spread_b())
    ky0, ky1 = send(y0, CORE), send(y1, CORE)
    rb = jnp.where((y == 0) & (z % 2 == 0), top, rb)
    r = jnp.concatenate([ra, rb], 0)
    xr = send(r, ASIDE)
    inv_k = send(inv, CORE)
    inv_ky = send(inv_y, CORE)
    sa, hi, lo = early(c, panel, mate, (inv, inv_k, inv_y, inv_ky))
    sb = late([widen(v) for v in (y0, y1, ky0, ky1)], hi, lo)
    here = x == k
    a = jnp.where(here, r[:NB], xr[:NB])
    b = jnp.where(here, r[NB:], xr[NB:])
    a_low = jnp.where(z % 2 == y, z >= 2, z < 2)
    ta = widen(jnp.where(a_low, a, b))
    tb = widen(jnp.where(a_low, b, a))
    return final(c, trailing, sa, sb, ta, tb, hi, lo)


def solution(mesh):
    in_specs = (P("row", "col"), P(("row", "col"), None), P(None, "col"))
    out_specs = P("row", "col")
    fits = mesh.shape["row"] == 8 and mesh.shape["col"] == 4
    return jax.shard_map(
        local_8x4 if fits else local_any,
        mesh=mesh,
        in_specs=in_specs,
        out_specs=out_specs,
        check_vma=False,
    )
```

time: 28.9 us -> 23.1 us (0.80)
  starting transfers between devices: 13.9 us -> 11.2 us
  waiting for transfers between devices: 6.89 us -> 5.09 us
  Pallas kernels: 4.44 us -> 3.19 us
    ppermute x13 -> x11, starting transfers between devices: 13.9 us -> 11.2 us  [send(): return lax.ppermute(value, AXES, pairs)]
    pallas_call x1, Pallas kernels: 3.83 us -> 2 us  [final(): pl.pallas_call(final_kernel, out_shape=jax.ShapeDtypeStruct((rows, cols),...]
    ppermute x13 -> x11, waiting for transfers between devices: 6.89 us -> 5.09 us  [send(): return lax.ppermute(value, AXES, pairs)]
    pallas_call x0 -> x1, Pallas kernels: none -> 0.58 us  [late(): pl.pallas_call(late_kernel, out_shape=jax.ShapeDtypeStruct((2, 2 * rest[0...]
  transfers between devices with their start and end apart: 13 -> 11, of which waited for: 4 -> 4; matrix products, arithmetic and copies ran while one was open for 5% -> 6% of each run, Pallas kernels for 2% -> 5%
where the time goes in v2:
time: 23.1 us; the launch traced here: 22.9 us
  starting transfers between devices  11.2 us (48%)
  waiting for transfers between devices  5.09 us (22%)
  Pallas kernels  3.19 us (14%)
  local copies, waits for them, and re-layouts  1.89 us (8%)
  other arithmetic  1.44 us (6%)
    ppermute x11, starting transfers between devices, send(): return lax.ppermute(value, AXES, pairs)  11.2 us
    ppermute x11, waiting for transfers between devices, send(): return lax.ppermute(value, AXES, pairs)  5.09 us
    pallas_call x1, Pallas kernels, final(): pl.pallas_call(final_kernel, out_shape=jax.ShapeDtypeStruct((rows, cols),...  2 us
    unnamed x6, local copies, waits for them, and re-layouts  1.89 us
    convert_element_type x1, other arithmetic, narrow(): return (value * SCALE).astype(F16)  1.12 us
    pallas_call x1, Pallas kernels, early(): pl.pallas_call(early_kernel, out_shape=(jax.ShapeDtypeStruct((2, n, NB),...  0.62 us
    pallas_call x1, Pallas kernels, late(): pl.pallas_call(late_kernel, out_shape=jax.ShapeDtypeStruct((2, 2 * rest[0...  0.58 us
  transfers between devices with their start and end apart: 11, of which 4 were waited for; matrix products, arithmetic and copies ran while one was open for 6% of the time, Pallas kernels for 5%

profile of v2, /device:TPU:0, one launch (start us, length us, event | category | flops | bytes accessed | tf_op | source)
XLA Modules:
  0.0 22.9 jit_solution(1893973118517130170)
XLA Ops:
  0.0 0.5 %collective-permute-start = (f32[512,256]{1,0:T(8,128)}, f32[512,256]{1,0:T(8,128)S(1)}, u32[]{:S(2)}, u32[]{:S(2)}) collective-permute-start(f32[512,256]{1,0:T(8,128)} %own_ref.1), channel_id=1, source_target_pairs={{0,1},{1,0},{2,3},{3,2},{4,5},{5,4},{6,7},{7,6},{8,9},{9,8},{10,11... | collective-permute-start | bytes 1572872 | tf_op jit(solution)/shard_map/ppermute | solution.py:90
  0.5 2.5 %collective-permute-start.2 = (f32[64,256]{1,0:T(8,128)}, f32[64,256]{1,0:T(8,128)S(1)}, u32[]{:S(2)}, u32[]{:S(2)}) collective-permute-start(f32[64,256]{1,0:T(8,128)} %bitcast.2), channel_id=1, source_target_pairs={{0,2},{1,3},{2,0},{3,1},{4,6},{5,7},{6,4},{7,5},{8,10},{9,11},{10,... | collective-permute-start | bytes 196616 | tf_op jit(solution)/shard_map/ppermute | solution.py:90
  3.0 0.0 collective-permute-done.mate_ref
  3.0 1.1 %fusion.1 = (f16[256,256]{1,0:T(8,128)(2,1)S(1)}, f16[256,256]{1,0:T(8,128)(2,1)S(1)}, f16[256,256]{1,0:T(8,128)(2,1)S(1)}) fusion(f32[512,256]{1,0:T(8,128)S(1)} %collective-permute-done.mate_ref, f32[512,256]{1,0:T(8,128)} %own_ref.1, pred[]{:T(512)S(6)} %eq.22), kind=kLoop, calls=%fused_computation.2 | loop fusion | flops 458752 | bytes 1179649 | tf_op jit(solution)/shard_map/convert_element_type | solution.py:203
  4.1 4.3 %collective-permute-start.9 = (f16[256,256]{1,0:T(8,128)(2,1)S(1)}, f16[256,256]{1,0:T(8,128)(2,1)S(1)}, u32[]{:S(2)}, u32[]{:S(2)}) collective-permute-start(f16[256,256]{1,0:T(8,128)(2,1)S(1)} %get-tuple-element.13), channel_id=1, source_target_pairs={{0,24},{1,0},{2,3},{3,1},{5,29},{4,5},{7,6},{6,4},{8,18},{9,10},{1... | collective-permute-start | bytes 393224 | tf_op jit(solution)/shard_map/ppermute | solution.py:90
  8.4 0.0 collective-permute-start.1
  8.4 0.0 collective-permute-done.2.l2
  8.4 0.5 %collective-permute-start.3 = (f32[64,256]{1,0:T(8,128)S(1)}, f32[64,256]{1,0:T(8,128)S(1)}, u32[]{:S(2)}, u32[]{:S(2)}) collective-permute-start(f32[64,256]{1,0:T(8,128)S(1)} %collective-permute-done.2.l2), channel_id=1, source_target_pairs={{0,1},{1,0},{2,3},{3,2},{4,5},{5,4},{6,7},{7,6},{8,9},{9,8},{10,11... | collective-permute-start | bytes 196616 | tf_op jit(solution)/shard_map/ppermute | solution.py:90
  8.9 0.5 %collective-permute-start.8 = (f16[256,256]{1,0:T(8,128)(2,1)S(1)}, f16[256,256]{1,0:T(8,128)(2,1)S(1)}, u32[]{:S(2)}, u32[]{:S(2)}) collective-permute-start(f16[256,256]{1,0:T(8,128)(2,1)S(1)} %get-tuple-element.13), channel_id=1, source_target_pairs={{0,8},{1,16},{2,3},{3,1},{5,13},{4,21},{7,6},{6,4},{8,2},{9,26},{1... | collective-permute-start | bytes 393224 | tf_op jit(solution)/shard_map/ppermute | solution.py:90
  9.4 0.0 collective-permute-start.5
  9.4 0.5 %collective-permute-done.1.l1 = f32[64,256]{1,0:T(8,128)S(1)} collective-permute-done((f32[64,256]{1,0:T(8,128)}, f32[64,256]{1,0:T(8,128)S(1)}, u32[]{:S(2)}, u32[]{:S(2)}) %collective-permute-start.1) | collective-permute-done | bytes 65568 | tf_op jit(solution)/shard_map/ppermute | solution.py:90
  9.8 1.6 %collective-permute-start.4 = (f16[256,256]{1,0:T(8,128)(2,1)S(1)}, f16[256,256]{1,0:T(8,128)(2,1)S(1)}, u32[]{:S(2)}, u32[]{:S(2)}) collective-permute-start(f16[256,256]{1,0:T(8,128)(2,1)S(1)} %get-tuple-element.15), channel_id=1, source_target_pairs={{0,2},{1,3},{2,0},{3,1},{4,6},{5,7},{6,4},{7,5},{8,10},{9,11},{10,... | collective-permute-start | bytes 393224 | tf_op jit(solution)/shard_map/ppermute | solution.py:90
  11.4 0.0 collective-permute-done.3.l3
  11.4 1.0 %copy-done.1 = f32[512,256]{1,0:T(8,128)S(1)} copy-done((f32[512,256]{1,0:T(8,128)S(1)}, f32[512,256]{1,0:T(8,128)}, u32[]{:S(2)}) %copy-start.1) | copy-done | bytes 524312
  12.5 0.8 %copy-done.2 = f32[256,64]{0,1:T(8,128)S(1)} copy-done((f32[256,64]{0,1:T(8,128)S(1)}, f32[256,64]{0,1:T(8,128)}, u32[]{:S(2)}) %copy-start.2) | copy-done | bytes 65560
  13.3 0.6 %shard_map.37 = (bf16[2,512,256]{2,1,0:T(8,128)(2,1)S(1)}, bf16[256,256]{1,0:T(8,128)(2,1)S(1)}, bf16[256,256]{1,0:T(8,128)(2,1)S(1)}) custom-call(s32[1]{0:T(128)} %bitcast.c_ref, f32[512,256]{1,0:T(8,128)S(1)} %copy-done.1, f32[512,256]{1,0:T(8,128)S(1)} %collective-permute-done.mate_ref, f32[64,256]{1,0:T(8,128)S(1)} %bitcast.4, ...), custom_call_target="tpu_custom_call" | custom-call | tf_op jit(solution)/shard_map/pallas_call | solution.py:126
  13.9 0.0 collective-permute-done.9
  14.0 1.3 %collective-permute-done.8 = f16[256,256]{1,0:T(8,128)(2,1)S(1)} collective-permute-done((f16[256,256]{1,0:T(8,128)(2,1)S(1)}, f16[256,256]{1,0:T(8,128)(2,1)S(1)}, u32[]{:S(2)}, u32[]{:S(2)}) %collective-permute-start.8) | collective-permute-done | bytes 131104 | tf_op jit(solution)/shard_map/ppermute | solution.py:90
  15.3 0.1 pad_maximum_fusion
  15.4 0.8 %collective-permute-start.10 = (f16[512,256]{1,0:T(8,128)(2,1)S(1)}, f16[512,256]{1,0:T(8,128)(2,1)S(1)}, u32[]{:S(2)}, u32[]{:S(2)}) collective-permute-start(f16[512,256]{1,0:T(8,128)(2,1)S(1)} %pad_maximum_fusion), channel_id=1, source_target_pairs={{0,4},{1,0},{2,6},{3,2},{4,5},{5,1},{6,7},{7,3},{8,12},{9,8},{10,1... | collective-permute-start | bytes 786440 | tf_op jit(solution)/shard_map/ppermute | solution.py:90
  16.2 2.3 %collective-permute-done.4 = f16[256,256]{1,0:T(8,128)(2,1)S(1)} collective-permute-done((f16[256,256]{1,0:T(8,128)(2,1)S(1)}, f16[256,256]{1,0:T(8,128)(2,1)S(1)}, u32[]{:S(2)}, u32[]{:S(2)}) %collective-permute-start.4) | collective-permute-done | bytes 131104 | tf_op jit(solution)/shard_map/ppermute | solution.py:90
  18.5 0.0 collective-permute-start.6
  18.5 0.0 copy-start
  18.5 0.0 collective-permute-done.5
  18.5 0.6 %collective-permute-start.7 = (f16[256,256]{1,0:T(8,128)(2,1)S(1)}, f16[256,256]{1,0:T(8,128)(2,1)S(1)}, u32[]{:S(2)}, u32[]{:S(2)}) collective-permute-start(f16[256,256]{1,0:T(8,128)(2,1)S(1)} %collective-permute-done.5), channel_id=1, source_target_pairs={{0,1},{1,0},{2,3},{3,2},{4,5},{5,4},{6,7},{7,6},{8,9},{9,8},{10,11... | collective-permute-start | bytes 393224 | tf_op jit(solution)/shard_map/ppermute | solution.py:90
  19.1 1.0 %collective-permute-done.7 = f16[256,256]{1,0:T(8,128)(2,1)S(1)} collective-permute-done((f16[256,256]{1,0:T(8,128)(2,1)S(1)}, f16[256,256]{1,0:T(8,128)(2,1)S(1)}, u32[]{:S(2)}, u32[]{:S(2)}) %collective-permute-start.7) | collective-permute-done | bytes 131104 | tf_op jit(solution)/shard_map/ppermute | solution.py:90
  20.1 0.0 collective-permute-done.6
  20.2 0.6 %shard_map.38.sb = bf16[2,512,256]{2,1,0:T(8,128)(2,1)S(1)} custom-call(f32[256,256]{1,0:T(8,128)S(1)} %convert_multiply_fusion.5.y0, f32[256,256]{1,0:T(8,128)S(1)} %convert_multiply_fusion.4.y1, f32[256,256]{1,0:T(8,128)S(1)} %convert_multiply_fusion.3.ky0, f32[256,256]{1,0:T(8,128)S(1)} %convert_multiply_fusion.2.ky1, ...), custom_call_target="tpu_custom_call" | custom-call | tf_op jit(solution)/shard_map/pallas_call | solution.py:150
  20.8 0.0 collective-permute-done.10
  20.8 0.1 convert_multiply_fusion
  20.9 0.0 copy-done
  20.9 2.0 %shard_map.39 = bf16[2048,512]{1,0:T(8,128)(2,1)} custom-call(s32[1]{0:T(128)} %bitcast.c_ref, bf16[2048,512]{1,0:T(8,128)(2,1)S(1)} %copy-done, bf16[2,512,256]{2,1,0:T(8,128)(2,1)S(1)} %get-tuple-element.8.sa, bf16[2,512,256]{2,1,0:T(8,128)(2,1)S(1)} %shard_map.38.sb, f32[256,256]{1,0:T(8,128)S(1)} %get-tuple-element.12.ta, ...), custom_call_target="tpu_custom_call" | custom-call | tf_op jit(solution)/shard_map/pallas_call | solution.py:184
  (7 shorter events, 0.1 us)
Async XLA Ops:
  0.0 3.0 %collective-permute-start = (f32[512,256]{1,0:T(8,128)}, f32[512,256]{1,0:T(8,128)S(1)}, u32[]{:S(2)}, u32[]{:S(2)}) collective-permute-start(f32[512,256]{1,0:T(8,128)} %own_ref.1), channel_id=1, source_target_pairs={{0,1},{1,0},{2,3},{3,2},{4,5},{5,4},{6,7},{7,6},{8,9},{9,8},{10,11... | collective-permute-start | bytes 1572872 | tf_op jit(solution)/shard_map/ppermute | solution.py:90
  0.5 7.9 %collective-permute-start.2 = (f32[64,256]{1,0:T(8,128)}, f32[64,256]{1,0:T(8,128)S(1)}, u32[]{:S(2)}, u32[]{:S(2)}) collective-permute-start(f32[64,256]{1,0:T(8,128)} %bitcast.2), channel_id=1, source_target_pairs={{0,2},{1,3},{2,0},{3,1},{4,6},{5,7},{6,4},{7,5},{8,10},{9,11},{10,... | collective-permute-start | bytes 196616 | tf_op jit(solution)/shard_map/ppermute | solution.py:90
  4.1 9.8 %collective-permute-start.9 = (f16[256,256]{1,0:T(8,128)(2,1)S(1)}, f16[256,256]{1,0:T(8,128)(2,1)S(1)}, u32[]{:S(2)}, u32[]{:S(2)}) collective-permute-start(f16[256,256]{1,0:T(8,128)(2,1)S(1)} %get-tuple-element.13), channel_id=1, source_target_pairs={{0,24},{1,0},{2,3},{3,1},{5,29},{4,5},{7,6},{6,4},{8,18},{9,10},{1... | collective-permute-start | bytes 393224 | tf_op jit(solution)/shard_map/ppermute | solution.py:90
  8.4 1.5 %collective-permute-start.1 = (f32[64,256]{1,0:T(8,128)}, f32[64,256]{1,0:T(8,128)S(1)}, u32[]{:S(2)}, u32[]{:S(2)}) collective-permute-start(f32[64,256]{1,0:T(8,128)} %bitcast.3), channel_id=1, source_target_pairs={{0,1},{1,0},{2,3},{3,2},{4,5},{5,4},{6,7},{7,6},{8,9},{9,8},{10,11... | collective-permute-start | bytes 196616 | tf_op jit(solution)/shard_map/ppermute | solution.py:90
  8.4 3.0 %collective-permute-start.3 = (f32[64,256]{1,0:T(8,128)S(1)}, f32[64,256]{1,0:T(8,128)S(1)}, u32[]{:S(2)}, u32[]{:S(2)}) collective-permute-start(f32[64,256]{1,0:T(8,128)S(1)} %collective-permute-done.2.l2), channel_id=1, source_target_pairs={{0,1},{1,0},{2,3},{3,2},{4,5},{5,4},{6,7},{7,6},{8,9},{9,8},{10,11... | collective-permute-start | bytes 196616 | tf_op jit(solution)/shard_map/ppermute | solution.py:90
  8.9 6.4 %collective-permute-start.8 = (f16[256,256]{1,0:T(8,128)(2,1)S(1)}, f16[256,256]{1,0:T(8,128)(2,1)S(1)}, u32[]{:S(2)}, u32[]{:S(2)}) collective-permute-start(f16[256,256]{1,0:T(8,128)(2,1)S(1)} %get-tuple-element.13), channel_id=1, source_target_pairs={{0,8},{1,16},{2,3},{3,1},{5,13},{4,21},{7,6},{6,4},{8,2},{9,26},{1... | collective-permute-start | bytes 393224 | tf_op jit(solution)/shard_map/ppermute | solution.py:90
  9.4 9.2 %collective-permute-start.5 = (f16[256,256]{1,0:T(8,128)(2,1)S(1)}, f16[256,256]{1,0:T(8,128)(2,1)S(1)}, u32[]{:S(2)}, u32[]{:S(2)}) collective-permute-start(f16[256,256]{1,0:T(8,128)(2,1)S(1)} %get-tuple-element.14), channel_id=1, source_target_pairs={{0,2},{1,3},{2,0},{3,1},{4,6},{5,7},{6,4},{7,5},{8,10},{9,11},{10,... | collective-permute-start | bytes 393224 | tf_op jit(solution)/shard_map/ppermute | solution.py:90
  9.8 8.6 %collective-permute-start.4 = (f16[256,256]{1,0:T(8,128)(2,1)S(1)}, f16[256,256]{1,0:T(8,128)(2,1)S(1)}, u32[]{:S(2)}, u32[]{:S(2)}) collective-permute-start(f16[256,256]{1,0:T(8,128)(2,1)S(1)} %get-tuple-element.15), channel_id=1, source_target_pairs={{0,2},{1,3},{2,0},{3,1},{4,6},{5,7},{6,4},{7,5},{8,10},{9,11},{10,... | collective-permute-start | bytes 393224 | tf_op jit(solution)/shard_map/ppermute | solution.py:90
  11.4 1.0 %copy-start.1 = (f32[512,256]{1,0:T(8,128)S(1)}, f32[512,256]{1,0:T(8,128)}, u32[]{:S(2)}) copy-start(f32[512,256]{1,0:T(8,128)} %own_ref.1) | copy-start | bytes 1572868
  12.5 0.8 %copy-start.2 = (f32[256,64]{0,1:T(8,128)S(1)}, f32[256,64]{0,1:T(8,128)}, u32[]{:S(2)}) copy-start(f32[256,64]{0,1:T(8,128)} %param.5) | copy-start | bytes 196612
  15.4 5.4 %collective-permute-start.10 = (f16[512,256]{1,0:T(8,128)(2,1)S(1)}, f16[512,256]{1,0:T(8,128)(2,1)S(1)}, u32[]{:S(2)}, u32[]{:S(2)}) collective-permute-start(f16[512,256]{1,0:T(8,128)(2,1)S(1)} %pad_maximum_fusion), channel_id=1, source_target_pairs={{0,4},{1,0},{2,6},{3,2},{4,5},{5,1},{6,7},{7,3},{8,12},{9,8},{10,1... | collective-permute-start | bytes 786440 | tf_op jit(solution)/shard_map/ppermute | solution.py:90
  18.5 1.6 %collective-permute-start.6 = (f16[256,256]{1,0:T(8,128)(2,1)S(1)}, f16[256,256]{1,0:T(8,128)(2,1)S(1)}, u32[]{:S(2)}, u32[]{:S(2)}) collective-permute-start(f16[256,256]{1,0:T(8,128)(2,1)S(1)} %collective-permute-done.4), channel_id=1, source_target_pairs={{0,1},{1,0},{2,3},{3,2},{4,5},{5,4},{6,7},{7,6},{8,9},{9,8},{10,11... | collective-permute-start | bytes 393224 | tf_op jit(solution)/shard_map/ppermute | solution.py:90
  18.5 2.4 %copy-start = (bf16[2048,512]{1,0:T(8,128)(2,1)S(1)}, bf16[2048,512]{1,0:T(8,128)(2,1)}, u32[]{:S(2)}) copy-start(bf16[2048,512]{1,0:T(8,128)(2,1)} %t_ref.1) | copy-start | bytes 6291460
  18.5 1.6 %collective-permute-start.7 = (f16[256,256]{1,0:T(8,128)(2,1)S(1)}, f16[256,256]{1,0:T(8,128)(2,1)S(1)}, u32[]{:S(2)}, u32[]{:S(2)}) collective-permute-start(f16[256,256]{1,0:T(8,128)(2,1)S(1)} %collective-permute-done.5), channel_id=1, source_target_pairs={{0,1},{1,0},{2,3},{3,2},{4,5},{5,4},{6,7},{7,6},{8,9},{9,8},{10,11... | collective-permute-start | bytes 393224 | tf_op jit(solution)/shard_map/ppermute | solution.py:90

commit v3 on v2

--- a/solution.py
+++ b/solution.py
@@ -8,6 +8,10 @@
 NB = 256
 SBLK = 2
 SCALE = 32768.0
+ORDER = (
+    ((0, 0), 0, 0), ((0, 1), 0, 1), ((0, 2), 1, 0), ((0, 3), 1, 1),
+    ((1, 0), 2, 0), ((1, 1), 2, 1), ((1, 2), 3, 0), ((1, 3), 3, 1),
+)
 AXES = ("row", "col")
 F32, F16, BF16 = jnp.float32, jnp.float16, jnp.bfloat16
 
@@ -104,7 +108,8 @@
     return (mul(hi, lt_hi) + (mul(hi, lt_lo) + mul(lo, lt_hi))).astype(BF16)
 
 
-def early_kernel(c_ref, own_ref, mate_ref, l0, l1, l2, l3, s_ref, hi_ref, lo_ref, lt_ref):
+def early_kernel(c_ref, l0, l1, l2, l3, *refs):
+    s_ref, hi_ref, lo_ref, lt_ref = refs[-4:]
     c = c_ref[0]
     for i, block in enumerate((l0, l1, l2, l3)):
         at = pl.multiple_of((c ^ i) * 64, 64)
@@ -112,8 +117,8 @@
     hi, lo = split(lt_ref[...])
     hi_ref[...] = hi
     lo_ref[...] = lo
-    s_ref[0] = solve(own_ref[...], hi, lo)
-    s_ref[1] = solve(mate_ref[...], hi, lo)
+    for i, rows in enumerate(refs[:-4]):
+        s_ref[2 * i : 2 * i + 2] = solve(rows[...], hi, lo).reshape(2, -1, NB)
 
 
 VMEM = pl.BlockSpec(memory_space=pltpu.VMEM)
@@ -121,52 +126,50 @@
 LIMIT = pltpu.CompilerParams(vmem_limit_bytes=24 * 1024 * 1024)
 
 
-def early(c, own, mate, blocks):
-    n = own.shape[0]
+def early(c, blocks, parts):
+    n = parts[0].shape[0]
     return pl.pallas_call(
         early_kernel,
         out_shape=(
-            jax.ShapeDtypeStruct((2, n, NB), BF16),
+            jax.ShapeDtypeStruct((2 * len(parts), n // 2, NB), BF16),
             jax.ShapeDtypeStruct((NB, NB), BF16),
             jax.ShapeDtypeStruct((NB, NB), BF16),
         ),
-        in_specs=[SMEM] + [VMEM] * 6,
+        in_specs=[SMEM] + [VMEM] * (4 + len(parts)),
         out_specs=(VMEM, VMEM, VMEM),
         scratch_shapes=[pltpu.VMEM((NB, NB), F32)],
         compiler_params=LIMIT,
-    )(c, own, mate, *blocks)
-
-
-def late_kernel(y0, y1, ky0, ky1, hi_ref, lo_ref, s_ref):
+    )(c, *blocks, *parts)
+
+
+def late_kernel(hi_ref, lo_ref, *refs):
     hi, lo = hi_ref[...], lo_ref[...]
-    half = y0.shape[0]
-    s_ref[0, :half] = solve(y0[...], hi, lo)
-    s_ref[0, half:] = solve(y1[...], hi, lo)
-    s_ref[1, :half] = solve(ky0[...], hi, lo)
-    s_ref[1, half:] = solve(ky1[...], hi, lo)
-
-
-def late(rest, hi, lo):
+    for i, rows in enumerate(refs[:-1]):
+        refs[-1][2 * i : 2 * i + 2] = solve(rows[...], hi, lo).reshape(2, -1, NB)
+
+
+def late(hi, lo, parts):
+    n = parts[0].shape[0]
     return pl.pallas_call(
         late_kernel,
-        out_shape=jax.ShapeDtypeStruct((2, 2 * rest[0].shape[0], NB), BF16),
-        in_specs=[VMEM] * 6,
+        out_shape=jax.ShapeDtypeStruct((2 * len(parts), n // 2, NB), BF16),
+        in_specs=[VMEM] * (2 + len(parts)),
         out_specs=VMEM,
         compiler_params=LIMIT,
-    )(*rest, hi, lo)
+    )(hi, lo, *parts)
 
 
 def final_kernel(c_ref, t_ref, sa, sb, ta, tb, hi_ref, lo_ref, o_ref, m_ref, buf, sems):
     c = c_ref[0]
-    n = sa.shape[1]
+    n = buf.shape[1]
     hi, lo = hi_ref[...], lo_ref[...]
     m_ref[:NB] = solve(ta[...], hi, lo)
     m_ref[NB:] = solve(tb[...], hi, lo)
     mirror = m_ref[...]
     copies = []
-    for i in range(4):
-        at = pl.multiple_of((c ^ i) * n, n)
-        rows = (sa if i < 2 else sb)[i % 2]
+    for i, (source, part, row) in enumerate(ORDER):
+        at = pl.multiple_of((c ^ part) * 2 * n + row * n, n)
+        rows = (sa, sb)[source[0]][source[1]]
         update = lax.dot_general(
             rows, mirror, (((1,), (1,)), ((), ())), preferred_element_type=F32
         )
@@ -180,7 +183,7 @@
 
 def final(c, trailing, sa, sb, ta, tb, hi, lo):
     rows, cols = trailing.shape
-    n = rows // 4
+    n = rows // 8
     return pl.pallas_call(
         final_kernel,
         out_shape=jax.ShapeDtypeStruct((rows, cols), BF16),
@@ -188,8 +191,8 @@
         out_specs=pl.BlockSpec(memory_space=pl.ANY),
         scratch_shapes=[
             pltpu.VMEM((2 * NB, NB), BF16),
-            pltpu.VMEM((4, n, cols), BF16),
-            pltpu.SemaphoreType.DMA((4,)),
+            pltpu.VMEM((8, n, cols), BF16),
+            pltpu.SemaphoreType.DMA((8,)),
         ],
         compiler_params=LIMIT,
     )(c, trailing, sa, sb, ta, tb, hi, lo)
@@ -212,18 +215,20 @@
 
     mate = send(panel, CORE)
     inv_y = send(inv, ACROSS)
-    y0 = send(narrow(panel[:NB]), ACROSS)
-    y1 = send(narrow(panel[NB:]), ACROSS)
-    top = narrow(jnp.where(k == 0, panel[:NB], mate[:NB]))
+    p, m = narrow(panel), narrow(mate)
+    top = jnp.where(k == 0, p[:NB], m[:NB])
+    p, m, top = barrier((p, m, top))
+    yp = send(p, ACROSS)
     ra, rb = send(top, spread_a()), send(top, spread_b())
-    ky0, ky1 = send(y0, CORE), send(y1, CORE)
-    rb = jnp.where((y == 0) & (z % 2 == 0), top, rb)
+    ra, rb, inv, inv_y = barrier((ra, rb, inv, inv_y))
+    inv_k = send(inv, CORE)
+    inv_ky = send(inv_y, CORE)
     r = jnp.concatenate([ra, rb], 0)
     xr = send(r, ASIDE)
-    inv_k = send(inv, CORE)
-    inv_ky = send(inv_y, CORE)
-    sa, hi, lo = early(c, panel, mate, (inv, inv_k, inv_y, inv_ky))
-    sb = late([widen(v) for v in (y0, y1, ky0, ky1)], hi, lo)
+    kyp = send(yp, CORE)
+    blocks = (inv, inv_k, inv_y, inv_ky)
+    sa, hi, lo = early(c, blocks, [widen(v) for v in (p, m)])
+    sb = late(hi, lo, [widen(v) for v in (yp, kyp)])
     here = x == k
     a = jnp.where(here, r[:NB], xr[:NB])
     b = jnp.where(here, r[NB:], xr[NB:])

time: 23.1 us -> 22.3 us (0.965)
  the two profiles are of different devices: /device:TPU:0 before, /device:TPU:1 now
where the time goes in v3:
time: 22.3 us; the launch traced here: 22.1 us
  starting transfers between devices  11.7 us (52%)
  waiting for transfers between devices  5.63 us (25%)
  Pallas kernels  3.18 us (14%)
  other arithmetic  1.53 us (7%)
    ppermute x9, starting transfers between devices, send(): return lax.ppermute(value, AXES, pairs)  11.7 us
    ppermute x9, waiting for transfers between devices, send(): return lax.ppermute(value, AXES, pairs)  5.63 us
    pallas_call x1, Pallas kernels, final(): pl.pallas_call(final_kernel, out_shape=jax.ShapeDtypeStruct((rows, cols),...  1.97 us
    convert_element_type x2, other arithmetic, narrow(): return (value * SCALE).astype(F16)  1.15 us
    pallas_call x1, Pallas kernels, early(): pl.pallas_call(early_kernel, out_shape=(jax.ShapeDtypeStruct((2 * len(par...  0.62 us
    pallas_call x1, Pallas kernels, late(): pl.pallas_call(late_kernel, out_shape=jax.ShapeDtypeStruct((2 * len(parts...  0.59 us
  transfers between devices with their start and end apart: 9, of which 6 were waited for; matrix products, arithmetic and copies ran while one was open for 6% of the time, Pallas kernels for 3%

profile of v3, /device:TPU:1, one launch (start us, length us, event | category | flops | bytes accessed | tf_op | source)
XLA Modules:
  0.0 22.1 jit_solution(5746550566993003839)
XLA Ops:
  0.0 0.0 copy-start.1
  0.0 0.1 collective-permute-start
  0.1 1.1 %multiply_convert_fusion.1 = f16[512,256]{1,0:T(8,128)(2,1)S(1)} fusion(f32[512,256]{1,0:T(8,128)} %param.4), kind=kLoop, calls=%fused_computation.5 | loop fusion | flops 262144 | bytes 786432 | tf_op jit(solution)/shard_map/convert_element_type | solution.py:206
  1.2 1.0 %collective-permute-done = f32[512,256]{1,0:T(8,128)S(1)} collective-permute-done((f32[512,256]{1,0:T(8,128)}, f32[512,256]{1,0:T(8,128)S(1)}, u32[]{:S(2)}, u32[]{:S(2)}) %collective-permute-start) | collective-permute-done | bytes 524320 | tf_op jit(solution)/shard_map/ppermute | solution.py:94
  2.1 0.1 multiply_convert_fusion
  2.2 0.2 collective-permute-start.2
  2.4 4.0 %collective-permute-start.1 = (f16[256,256]{1,0:T(8,128)(2,1)S(1)}, f16[256,256]{1,0:T(8,128)(2,1)S(1)}, u32[]{:S(2)}, u32[]{:S(2)}) collective-permute-start(f16[256,256]{1,0:T(8,128)(2,1)S(1)} %slice_select_fusion.2), channel_id=1, source_target_pairs={{0,8},{1,16},{2,3},{3,1},{5,13},{4,21},{7,6},{6,4},{8,2},{9,26},{1... | collective-permute-start | bytes 393224 | tf_op jit(solution)/shard_map/ppermute | solution.py:94
  6.4 0.0 collective-permute-start.3
  6.4 1.5 %collective-permute-start.6 = (f16[512,256]{1,0:T(8,128)(2,1)S(1)}, f16[512,256]{1,0:T(8,128)(2,1)S(1)}, u32[]{:S(2)}, u32[]{:S(2)}) collective-permute-start(f16[512,256]{1,0:T(8,128)(2,1)S(1)} %multiply_convert_fusion.1), channel_id=1, source_target_pairs={{0,2},{1,3},{2,0},{3,1},{4,6},{5,7},{6,4},{7,5},{8,10},{9,11},{10,... | collective-permute-start | bytes 786440 | tf_op jit(solution)/shard_map/ppermute | solution.py:94
  7.9 1.9 %collective-permute-done.3.l2 = f32[64,256]{1,0:T(8,128)S(1)} collective-permute-done((f32[64,256]{1,0:T(8,128)}, f32[64,256]{1,0:T(8,128)S(1)}, u32[]{:S(2)}, u32[]{:S(2)}) %collective-permute-start.3) | collective-permute-done | bytes 65568 | tf_op jit(solution)/shard_map/ppermute | solution.py:94
  9.8 0.0 collective-permute-done.2
  9.8 0.0 collective-permute-done.1
  9.8 4.3 %collective-permute-start.4 = (f32[64,256]{1,0:T(8,128)}, f32[64,256]{1,0:T(8,128)S(1)}, u32[]{:S(2)}, u32[]{:S(2)}) collective-permute-start(f32[64,256]{1,0:T(8,128)} %bitcast.3), channel_id=1, source_target_pairs={{0,1},{1,0},{2,3},{3,2},{4,5},{5,4},{6,7},{7,6},{8,9},{9,8},{10,11... | collective-permute-start | bytes 196616 | tf_op jit(solution)/shard_map/ppermute | solution.py:94
  14.1 0.0 collective-permute-start.5
  14.1 0.1 pad_maximum_fusion
  14.2 0.5 %collective-permute-start.8 = (f16[512,256]{1,0:T(8,128)(2,1)S(1)}, f16[512,256]{1,0:T(8,128)(2,1)S(1)}, u32[]{:S(2)}, u32[]{:S(2)}) collective-permute-start(f16[512,256]{1,0:T(8,128)(2,1)S(1)} %pad_maximum_fusion), channel_id=1, source_target_pairs={{0,4},{1,0},{2,6},{3,2},{4,5},{5,1},{6,7},{7,3},{8,12},{9,8},{10,1... | collective-permute-start | bytes 786440 | tf_op jit(solution)/shard_map/ppermute | solution.py:94
  14.7 0.1 convert_multiply_fusion.2
  14.8 0.5 %collective-permute-done.4.l1 = f32[64,256]{1,0:T(8,128)S(1)} collective-permute-done((f32[64,256]{1,0:T(8,128)}, f32[64,256]{1,0:T(8,128)S(1)}, u32[]{:S(2)}, u32[]{:S(2)}) %collective-permute-start.4) | collective-permute-done | bytes 65568 | tf_op jit(solution)/shard_map/ppermute | solution.py:94
  15.2 0.1 collective-permute-done.5.l3
  15.4 0.0 copy-done.1
  15.4 0.6 %shard_map.37 = (bf16[4,256,256]{2,1,0:T(8,128)(2,1)S(1)}, bf16[256,256]{1,0:T(8,128)(2,1)S(1)}, bf16[256,256]{1,0:T(8,128)(2,1)S(1)}) custom-call(s32[1]{0:T(128)} %bitcast.c_ref, f32[64,256]{1,0:T(8,128)S(1)} %bitcast.4, f32[64,256]{1,0:T(8,128)S(1)} %collective-permute-done.4.l1, f32[64,256]{1,0:T(8,128)S(1)} %collective-permute-done.3.l2, ...), custom_call_target="tpu_custom_call" | custom-call | tf_op jit(solution)/shard_map/pallas_call | solution.py:131
  16.0 0.0 copy-start
  16.0 0.4 %collective-permute-done.6 = f16[512,256]{1,0:T(8,128)(2,1)S(1)} collective-permute-done((f16[512,256]{1,0:T(8,128)(2,1)S(1)}, f16[512,256]{1,0:T(8,128)(2,1)S(1)}, u32[]{:S(2)}, u32[]{:S(2)}) %collective-permute-start.6) | collective-permute-done | bytes 262176 | tf_op jit(solution)/shard_map/ppermute | solution.py:94
  16.4 1.1 %collective-permute-start.7 = (f16[512,256]{1,0:T(8,128)(2,1)S(1)}, f16[512,256]{1,0:T(8,128)(2,1)S(1)}, u32[]{:S(2)}, u32[]{:S(2)}) collective-permute-start(f16[512,256]{1,0:T(8,128)(2,1)S(1)} %collective-permute-done.6), channel_id=1, source_target_pairs={{0,1},{1,0},{2,3},{3,2},{4,5},{5,4},{6,7},{7,6},{8,9},{9,8},{10,11... | collective-permute-start | bytes 786440 | tf_op jit(solution)/shard_map/ppermute | solution.py:94
  17.6 1.8 %collective-permute-done.8 = f16[512,256]{1,0:T(8,128)(2,1)S(1)} collective-permute-done((f16[512,256]{1,0:T(8,128)(2,1)S(1)}, f16[512,256]{1,0:T(8,128)(2,1)S(1)}, u32[]{:S(2)}, u32[]{:S(2)}) %collective-permute-start.8) | collective-permute-done | bytes 262176 | tf_op jit(solution)/shard_map/ppermute | solution.py:94
  19.4 0.1 convert_multiply_fusion.4
  19.5 0.0 collective-permute-done.7
  19.6 0.6 %shard_map.38.sb = bf16[4,256,256]{2,1,0:T(8,128)(2,1)S(1)} custom-call(bf16[256,256]{1,0:T(8,128)(2,1)S(1)} %get-tuple-element.21.hi_ref, bf16[256,256]{1,0:T(8,128)(2,1)S(1)} %get-tuple-element.22.lo_ref, f32[512,256]{1,0:T(8,128)S(1)} %convert_multiply_fusion.1.refs_0_, f32[512,256]{1,0:T(8,128)S(1)} %convert_multiply_fusion.refs_1_), custom_call_target="tpu_custom_call" | custom-call | tf_op jit(solution)/shard_map/pallas_call | solution.py:153
  20.2 0.0 copy-done
  20.2 2.0 %shard_map.39 = bf16[2048,512]{1,0:T(8,128)(2,1)} custom-call(s32[1]{0:T(128)} %bitcast.c_ref, bf16[2048,512]{1,0:T(8,128)(2,1)S(1)} %copy-done, bf16[4,256,256]{2,1,0:T(8,128)(2,1)S(1)} %get-tuple-element.20.sa, bf16[4,256,256]{2,1,0:T(8,128)(2,1)S(1)} %shard_map.38.sb, f32[256,256]{1,0:T(8,128)S(1)} %get-tuple-element.26.ta, ...), custom_call_target="tpu_custom_call" | custom-call | tf_op jit(solution)/shard_map/pallas_call | solution.py:187
  (3 shorter events, 0.1 us)
Async XLA Ops:
  0.0 15.4 %copy-start.1 = (f32[256,64]{0,1:T(8,128)S(1)}, f32[256,64]{0,1:T(8,128)}, u32[]{:S(2)}) copy-start(f32[256,64]{0,1:T(8,128)} %param.5) | copy-start | bytes 196612
  0.0 2.1 %collective-permute-start = (f32[512,256]{1,0:T(8,128)}, f32[512,256]{1,0:T(8,128)S(1)}, u32[]{:S(2)}, u32[]{:S(2)}) collective-permute-start(f32[512,256]{1,0:T(8,128)} %param.4), channel_id=1, source_target_pairs={{0,1},{1,0},{2,3},{3,2},{4,5},{5,4},{6,7},{7,6},{8,9},{9,8},{10,11... | collective-permute-start | bytes 1572872 | tf_op jit(solution)/shard_map/ppermute | solution.py:94
  2.2 7.5 %collective-permute-start.2 = (f16[256,256]{1,0:T(8,128)(2,1)S(1)}, f16[256,256]{1,0:T(8,128)(2,1)S(1)}, u32[]{:S(2)}, u32[]{:S(2)}) collective-permute-start(f16[256,256]{1,0:T(8,128)(2,1)S(1)} %slice_select_fusion.2), channel_id=1, source_target_pairs={{0,24},{1,0},{2,3},{3,1},{5,29},{4,5},{7,6},{6,4},{8,18},{9,10},{1... | collective-permute-start | bytes 393224 | tf_op jit(solution)/shard_map/ppermute | solution.py:94
  2.4 7.3 %collective-permute-start.1 = (f16[256,256]{1,0:T(8,128)(2,1)S(1)}, f16[256,256]{1,0:T(8,128)(2,1)S(1)}, u32[]{:S(2)}, u32[]{:S(2)}) collective-permute-start(f16[256,256]{1,0:T(8,128)(2,1)S(1)} %slice_select_fusion.2), channel_id=1, source_target_pairs={{0,8},{1,16},{2,3},{3,1},{5,13},{4,21},{7,6},{6,4},{8,2},{9,26},{1... | collective-permute-start | bytes 393224 | tf_op jit(solution)/shard_map/ppermute | solution.py:94
  6.4 3.3 %collective-permute-start.3 = (f32[64,256]{1,0:T(8,128)}, f32[64,256]{1,0:T(8,128)S(1)}, u32[]{:S(2)}, u32[]{:S(2)}) collective-permute-start(f32[64,256]{1,0:T(8,128)} %bitcast.2), channel_id=1, source_target_pairs={{0,2},{1,3},{2,0},{3,1},{4,6},{5,7},{6,4},{7,5},{8,10},{9,11},{10,... | collective-permute-start | bytes 196616 | tf_op jit(solution)/shard_map/ppermute | solution.py:94
  6.4 10.0 %collective-permute-start.6 = (f16[512,256]{1,0:T(8,128)(2,1)S(1)}, f16[512,256]{1,0:T(8,128)(2,1)S(1)}, u32[]{:S(2)}, u32[]{:S(2)}) collective-permute-start(f16[512,256]{1,0:T(8,128)(2,1)S(1)} %multiply_convert_fusion.1), channel_id=1, source_target_pairs={{0,2},{1,3},{2,0},{3,1},{4,6},{5,7},{6,4},{7,5},{8,10},{9,11},{10,... | collective-permute-start | bytes 786440 | tf_op jit(solution)/shard_map/ppermute | solution.py:94
  9.8 5.5 %collective-permute-start.4 = (f32[64,256]{1,0:T(8,128)}, f32[64,256]{1,0:T(8,128)S(1)}, u32[]{:S(2)}, u32[]{:S(2)}) collective-permute-start(f32[64,256]{1,0:T(8,128)} %bitcast.3), channel_id=1, source_target_pairs={{0,1},{1,0},{2,3},{3,2},{4,5},{5,4},{6,7},{7,6},{8,9},{9,8},{10,11... | collective-permute-start | bytes 196616 | tf_op jit(solution)/shard_map/ppermute | solution.py:94
  14.1 1.3 %collective-permute-start.5 = (f32[64,256]{1,0:T(8,128)S(1)}, f32[64,256]{1,0:T(8,128)S(1)}, u32[]{:S(2)}, u32[]{:S(2)}) collective-permute-start(f32[64,256]{1,0:T(8,128)S(1)} %collective-permute-done.3.l2), channel_id=1, source_target_pairs={{0,1},{1,0},{2,3},{3,2},{4,5},{5,4},{6,7},{7,6},{8,9},{9,8},{10,11... | collective-permute-start | bytes 196616 | tf_op jit(solution)/shard_map/ppermute | solution.py:94
  14.2 5.2 %collective-permute-start.8 = (f16[512,256]{1,0:T(8,128)(2,1)S(1)}, f16[512,256]{1,0:T(8,128)(2,1)S(1)}, u32[]{:S(2)}, u32[]{:S(2)}) collective-permute-start(f16[512,256]{1,0:T(8,128)(2,1)S(1)} %pad_maximum_fusion), channel_id=1, source_target_pairs={{0,4},{1,0},{2,6},{3,2},{4,5},{5,1},{6,7},{7,3},{8,12},{9,8},{10,1... | collective-permute-start | bytes 786440 | tf_op jit(solution)/shard_map/ppermute | solution.py:94
  16.0 4.2 %copy-start = (bf16[2048,512]{1,0:T(8,128)(2,1)S(1)}, bf16[2048,512]{1,0:T(8,128)(2,1)}, u32[]{:S(2)}) copy-start(bf16[2048,512]{1,0:T(8,128)(2,1)} %t_ref.1) | copy-start | bytes 6291460
  16.4 3.1 %collective-permute-start.7 = (f16[512,256]{1,0:T(8,128)(2,1)S(1)}, f16[512,256]{1,0:T(8,128)(2,1)S(1)}, u32[]{:S(2)}, u32[]{:S(2)}) collective-permute-start(f16[512,256]{1,0:T(8,128)(2,1)S(1)} %collective-permute-done.6), channel_id=1, source_target_pairs={{0,1},{1,0},{2,3},{3,2},{4,5},{5,4},{6,7},{7,6},{8,9},{9,8},{10,11... | collective-permute-start | bytes 786440 | tf_op jit(solution)/shard_map/ppermute | solution.py:94

commit v4 on v3

--- a/solution.py
+++ b/solution.py
@@ -118,7 +118,7 @@
     hi_ref[...] = hi
     lo_ref[...] = lo
     for i, rows in enumerate(refs[:-4]):
-        s_ref[2 * i : 2 * i + 2] = solve(rows[...], hi, lo).reshape(2, -1, NB)
+        s_ref[i] = solve(rows[...], hi, lo)
 
 
 VMEM = pl.BlockSpec(memory_space=pltpu.VMEM)
@@ -131,7 +131,7 @@
     return pl.pallas_call(
         early_kernel,
         out_shape=(
-            jax.ShapeDtypeStruct((2 * len(parts), n // 2, NB), BF16),
+            jax.ShapeDtypeStruct((len(parts), n, NB), BF16),
             jax.ShapeDtypeStruct((NB, NB), BF16),
             jax.ShapeDtypeStruct((NB, NB), BF16),
         ),
@@ -145,14 +145,14 @@
 def late_kernel(hi_ref, lo_ref, *refs):
     hi, lo = hi_ref[...], lo_ref[...]
     for i, rows in enumerate(refs[:-1]):
-        refs[-1][2 * i : 2 * i + 2] = solve(rows[...], hi, lo).reshape(2, -1, NB)
+        refs[-1][i] = solve(rows[...], hi, lo)
 
 
 def late(hi, lo, parts):
     n = parts[0].shape[0]
     return pl.pallas_call(
         late_kernel,
-        out_shape=jax.ShapeDtypeStruct((2 * len(parts), n // 2, NB), BF16),
+        out_shape=jax.ShapeDtypeStruct((len(parts), n, NB), BF16),
         in_specs=[VMEM] * (2 + len(parts)),
         out_specs=VMEM,
         compiler_params=LIMIT,
@@ -218,17 +218,18 @@
     p, m = narrow(panel), narrow(mate)
     top = jnp.where(k == 0, p[:NB], m[:NB])
     p, m, top = barrier((p, m, top))
-    yp = send(p, ACROSS)
+    y0, y1 = send(p[:NB], ACROSS), send(p[NB:], ACROSS)
     ra, rb = send(top, spread_a()), send(top, spread_b())
-    ra, rb, inv, inv_y = barrier((ra, rb, inv, inv_y))
-    inv_k = send(inv, CORE)
-    inv_ky = send(inv_y, CORE)
     r = jnp.concatenate([ra, rb], 0)
     xr = send(r, ASIDE)
-    kyp = send(yp, CORE)
+    inv_y, inv, *_ = barrier((inv_y, inv, r))
+    y0, y1, *_ = barrier((y0, y1, r))
+    inv_k, inv_ky = send(inv, CORE), send(inv_y, CORE)
+    ky0, ky1 = send(y0, CORE), send(y1, CORE)
     blocks = (inv, inv_k, inv_y, inv_ky)
-    sa, hi, lo = early(c, blocks, [widen(v) for v in (p, m)])
-    sb = late(hi, lo, [widen(v) for v in (yp, kyp)])
+    s, hi, lo = early(c, blocks, [widen(v) for v in (p[:NB], p[NB:], m[:NB], m[NB:])])
+    sb = late(hi, lo, [widen(v) for v in (y0, y1, ky0, ky1)])
+    sa = s
     here = x == k
     a = jnp.where(here, r[:NB], xr[:NB])
     b = jnp.where(here, r[NB:], xr[NB:])

time: 22.3 us -> 21.3 us (0.955)
  the two profiles are of different devices: /device:TPU:1 before, /device:TPU:0 now
where the time goes in v4:
time: 21.3 us; the launch traced here: 21.1 us
  starting transfers between devices  9.83 us (46%)
  waiting for transfers between devices  5.84 us (27%)
  Pallas kernels  3.16 us (15%)
  other arithmetic  1.48 us (7%)
  local copies, waits for them, and re-layouts  0.64 us (3%)
    ppermute x11, starting transfers between devices, send(): return lax.ppermute(value, AXES, pairs)  9.83 us
    ppermute x11, waiting for transfers between devices, send(): return lax.ppermute(value, AXES, pairs)  5.84 us
    pallas_call x1, Pallas kernels, final(): pl.pallas_call(final_kernel, out_shape=jax.ShapeDtypeStruct((rows, cols),...  1.96 us
    convert_element_type x2, other arithmetic, narrow(): return (value * SCALE).astype(F16)  1.15 us
    pallas_call x1, Pallas kernels, early(): pl.pallas_call(early_kernel, out_shape=(jax.ShapeDtypeStruct((len(parts),...  0.62 us
    pallas_call x1, Pallas kernels, late(): pl.pallas_call(late_kernel, out_shape=jax.ShapeDtypeStruct((len(parts), n...  0.59 us
    unnamed x5, local copies, waits for them, and re-layouts  0.57 us
  transfers between devices with their start and end apart: 11, of which 4 were waited for; matrix products, arithmetic and copies ran while one was open for 7% of the time, Pallas kernels for 6%

profile of v4, /device:TPU:0, one launch (start us, length us, event | category | flops | bytes accessed | tf_op | source)
XLA Modules:
  0.0 21.1 jit_solution(4025688694383222139)
XLA Ops:
  0.0 0.5 %collective-permute-start.1 = (f32[512,256]{1,0:T(8,128)}, f32[512,256]{1,0:T(8,128)S(1)}, u32[]{:S(2)}, u32[]{:S(2)}) collective-permute-start(f32[512,256]{1,0:T(8,128)} %param.4), channel_id=1, source_target_pairs={{0,1},{1,0},{2,3},{3,2},{4,5},{5,4},{6,7},{7,6},{8,9},{9,8},{10,11... | collective-permute-start | bytes 1572872 | tf_op jit(solution)/shard_map/ppermute | solution.py:94
  0.5 2.5 %collective-permute-start = (f32[64,256]{1,0:T(8,128)}, f32[64,256]{1,0:T(8,128)S(1)}, u32[]{:S(2)}, u32[]{:S(2)}) collective-permute-start(f32[64,256]{1,0:T(8,128)} %bitcast.2), channel_id=1, source_target_pairs={{0,2},{1,3},{2,0},{3,1},{4,6},{5,7},{6,4},{7,5},{8,10},{9,11},{10,... | collective-permute-start | bytes 196616 | tf_op jit(solution)/shard_map/ppermute | solution.py:94
  3.0 1.1 %multiply_convert_fusion.1 = f16[512,256]{1,0:T(8,128)(2,1)S(1)} fusion(f32[512,256]{1,0:T(8,128)} %param.4), kind=kLoop, calls=%fused_computation.1 | loop fusion | flops 262144 | bytes 786432 | tf_op jit(solution)/shard_map/convert_element_type | solution.py:206
  4.1 0.0 copy-start.1
  4.1 0.0 collective-permute-done.1
  4.1 0.1 multiply_convert_fusion
  4.2 3.7 %collective-permute-start.3 = (f16[256,256]{1,0:T(8,128)(2,1)S(1)}, f16[256,256]{1,0:T(8,128)(2,1)S(1)}, u32[]{:S(2)}, u32[]{:S(2)}) collective-permute-start(f16[256,256]{1,0:T(8,128)(2,1)S(1)} %slice_select_fusion.2), channel_id=1, source_target_pairs={{0,24},{1,0},{2,3},{3,1},{5,29},{4,5},{7,6},{6,4},{8,18},{9,10},{1... | collective-permute-start | bytes 393224 | tf_op jit(solution)/shard_map/ppermute | solution.py:94
  7.9 0.0 collective-permute-start.2
  7.9 0.1 collective-permute-start.7
  8.0 2.0 %collective-permute-start.6 = (f16[256,256]{1,0:T(8,128)(2,1)S(1)}, f16[256,256]{1,0:T(8,128)(2,1)S(1)}, u32[]{:S(2)}, u32[]{:S(2)}) collective-permute-start(f16[256,256]{1,0:T(8,128)(2,1)S(1)} %get-tuple-element.28), channel_id=1, source_target_pairs={{0,2},{1,3},{2,0},{3,1},{4,6},{5,7},{6,4},{7,5},{8,10},{9,11},{10,... | collective-permute-start | bytes 393224 | tf_op jit(solution)/shard_map/ppermute | solution.py:94
  10.0 0.1 convert_multiply_fusion.6
  10.1 4.3 %collective-permute-done.2 = f16[256,256]{1,0:T(8,128)(2,1)S(1)} collective-permute-done((f16[256,256]{1,0:T(8,128)(2,1)S(1)}, f16[256,256]{1,0:T(8,128)(2,1)S(1)}, u32[]{:S(2)}, u32[]{:S(2)}) %collective-permute-start.2) | collective-permute-done | bytes 131104 | tf_op jit(solution)/shard_map/ppermute | solution.py:94
  14.5 0.0 collective-permute-done.3
  14.5 0.0 collective-permute-start.10
  14.6 0.0 collective-permute-done.l2
  14.6 0.5 %collective-permute-start.4 = (f32[64,256]{1,0:T(8,128)S(1)}, f32[64,256]{1,0:T(8,128)S(1)}, u32[]{:S(2)}, u32[]{:S(2)}) collective-permute-start(f32[64,256]{1,0:T(8,128)S(1)} %bitcast.3), channel_id=1, source_target_pairs={{0,1},{1,0},{2,3},{3,2},{4,5},{5,4},{6,7},{7,6},{8,9},{9,8},{10,11... | collective-permute-start | bytes 196616 | tf_op jit(solution)/shard_map/ppermute | solution.py:94
  15.1 0.1 collective-permute-start.5
  15.2 0.0 collective-permute-done.7
  15.2 1.2 %collective-permute-done.6 = f16[256,256]{1,0:T(8,128)(2,1)S(1)} collective-permute-done((f16[256,256]{1,0:T(8,128)(2,1)S(1)}, f16[256,256]{1,0:T(8,128)(2,1)S(1)}, u32[]{:S(2)}, u32[]{:S(2)}) %collective-permute-start.6) | collective-permute-done | bytes 131104 | tf_op jit(solution)/shard_map/ppermute | solution.py:94
  16.4 0.0 collective-permute-start.8
  16.4 0.5 %collective-permute-start.9 = (f16[256,256]{1,0:T(8,128)(2,1)S(1)}, f16[256,256]{1,0:T(8,128)(2,1)S(1)}, u32[]{:S(2)}, u32[]{:S(2)}) collective-permute-start(f16[256,256]{1,0:T(8,128)(2,1)S(1)} %collective-permute-done.7), channel_id=1, source_target_pairs={{0,1},{1,0},{2,3},{3,2},{4,5},{5,4},{6,7},{7,6},{8,9},{9,8},{10,11... | collective-permute-start | bytes 393224 | tf_op jit(solution)/shard_map/ppermute | solution.py:94
  16.9 0.0 collective-permute-done.4.l1
  16.9 0.0 collective-permute-done.5.l3
  16.9 0.6 %shard_map.37 = (bf16[4,256,256]{2,1,0:T(8,128)(2,1)S(1)}, bf16[256,256]{1,0:T(8,128)(2,1)S(1)}, bf16[256,256]{1,0:T(8,128)(2,1)S(1)}) custom-call(s32[1]{0:T(128)} %bitcast.c_ref, f32[64,256]{1,0:T(8,128)S(1)} %bitcast.4, f32[64,256]{1,0:T(8,128)S(1)} %collective-permute-done.4.l1, f32[64,256]{1,0:T(8,128)S(1)} %collective-permute-done.l2, ...), custom_call_target="tpu_custom_call" | custom-call | tf_op jit(solution)/shard_map/pallas_call | solution.py:131
  17.6 0.0 copy-start
  17.6 0.1 collective-permute-done.8
  17.7 0.2 collective-permute-done.9
  17.9 0.6 %shard_map.38.sb = bf16[4,256,256]{2,1,0:T(8,128)(2,1)S(1)} custom-call(bf16[256,256]{1,0:T(8,128)(2,1)S(1)} %get-tuple-element.21.hi_ref, bf16[256,256]{1,0:T(8,128)(2,1)S(1)} %get-tuple-element.22.lo_ref, f32[256,256]{1,0:T(8,128)S(1)} %get-tuple-element.36.refs_0_, f32[256,256]{1,0:T(8,128)S(1)} %get-tuple-element.35.refs_1_, ...), custom_call_target="tpu_custom_call" | custom-call | tf_op jit(solution)/shard_map/pallas_call | solution.py:153
  18.5 0.0 collective-permute-done.10
  18.5 0.1 convert_multiply_fusion
  18.6 0.5 %copy-done = bf16[2048,512]{1,0:T(8,128)(2,1)S(1)} copy-done((bf16[2048,512]{1,0:T(8,128)(2,1)S(1)}, bf16[2048,512]{1,0:T(8,128)(2,1)}, u32[]{:S(2)}) %copy-start) | copy-done | bytes 2097176
  19.2 2.0 %shard_map.39 = bf16[2048,512]{1,0:T(8,128)(2,1)} custom-call(s32[1]{0:T(128)} %bitcast.c_ref, bf16[2048,512]{1,0:T(8,128)(2,1)S(1)} %copy-done, bf16[4,256,256]{2,1,0:T(8,128)(2,1)S(1)} %get-tuple-element.20.sa, bf16[4,256,256]{2,1,0:T(8,128)(2,1)S(1)} %shard_map.38.sb, f32[256,256]{1,0:T(8,128)S(1)} %get-tuple-element.26.ta, ...), custom_call_target="tpu_custom_call" | custom-call | tf_op jit(solution)/shard_map/pallas_call | solution.py:187
  (8 shorter events, 0.2 us)
Async XLA Ops:
  0.0 4.1 %collective-permute-start.1 = (f32[512,256]{1,0:T(8,128)}, f32[512,256]{1,0:T(8,128)S(1)}, u32[]{:S(2)}, u32[]{:S(2)}) collective-permute-start(f32[512,256]{1,0:T(8,128)} %param.4), channel_id=1, source_target_pairs={{0,1},{1,0},{2,3},{3,2},{4,5},{5,4},{6,7},{7,6},{8,9},{9,8},{10,11... | collective-permute-start | bytes 1572872 | tf_op jit(solution)/shard_map/ppermute | solution.py:94
  0.5 14.1 %collective-permute-start = (f32[64,256]{1,0:T(8,128)}, f32[64,256]{1,0:T(8,128)S(1)}, u32[]{:S(2)}, u32[]{:S(2)}) collective-permute-start(f32[64,256]{1,0:T(8,128)} %bitcast.2), channel_id=1, source_target_pairs={{0,2},{1,3},{2,0},{3,1},{4,6},{5,7},{6,4},{7,5},{8,10},{9,11},{10,... | collective-permute-start | bytes 196616 | tf_op jit(solution)/shard_map/ppermute | solution.py:94
  4.1 10.5 %copy-start.1 = (f32[256,64]{0,1:T(8,128)S(1)}, f32[256,64]{0,1:T(8,128)}, u32[]{:S(2)}) copy-start(f32[256,64]{0,1:T(8,128)} %param.5) | copy-start | bytes 196612
  4.2 10.3 %collective-permute-start.3 = (f16[256,256]{1,0:T(8,128)(2,1)S(1)}, f16[256,256]{1,0:T(8,128)(2,1)S(1)}, u32[]{:S(2)}, u32[]{:S(2)}) collective-permute-start(f16[256,256]{1,0:T(8,128)(2,1)S(1)} %slice_select_fusion.2), channel_id=1, source_target_pairs={{0,24},{1,0},{2,3},{3,1},{5,29},{4,5},{7,6},{6,4},{8,18},{9,10},{1... | collective-permute-start | bytes 393224 | tf_op jit(solution)/shard_map/ppermute | solution.py:94
  7.9 6.6 %collective-permute-start.2 = (f16[256,256]{1,0:T(8,128)(2,1)S(1)}, f16[256,256]{1,0:T(8,128)(2,1)S(1)}, u32[]{:S(2)}, u32[]{:S(2)}) collective-permute-start(f16[256,256]{1,0:T(8,128)(2,1)S(1)} %slice_select_fusion.2), channel_id=1, source_target_pairs={{0,8},{1,16},{2,3},{3,1},{5,13},{4,21},{7,6},{6,4},{8,2},{9,26},{1... | collective-permute-start | bytes 393224 | tf_op jit(solution)/shard_map/ppermute | solution.py:94
  7.9 7.2 %collective-permute-start.7 = (f16[256,256]{1,0:T(8,128)(2,1)S(1)}, f16[256,256]{1,0:T(8,128)(2,1)S(1)}, u32[]{:S(2)}, u32[]{:S(2)}) collective-permute-start(f16[256,256]{1,0:T(8,128)(2,1)S(1)} %get-tuple-element.27), channel_id=1, source_target_pairs={{0,2},{1,3},{2,0},{3,1},{4,6},{5,7},{6,4},{7,5},{8,10},{9,11},{10,... | collective-permute-start | bytes 393224 | tf_op jit(solution)/shard_map/ppermute | solution.py:94
  8.0 8.4 %collective-permute-start.6 = (f16[256,256]{1,0:T(8,128)(2,1)S(1)}, f16[256,256]{1,0:T(8,128)(2,1)S(1)}, u32[]{:S(2)}, u32[]{:S(2)}) collective-permute-start(f16[256,256]{1,0:T(8,128)(2,1)S(1)} %get-tuple-element.28), channel_id=1, source_target_pairs={{0,2},{1,3},{2,0},{3,1},{4,6},{5,7},{6,4},{7,5},{8,10},{9,11},{10,... | collective-permute-start | bytes 393224 | tf_op jit(solution)/shard_map/ppermute | solution.py:94
  14.5 4.0 %collective-permute-start.10 = (f16[512,256]{1,0:T(8,128)(2,1)S(1)}, f16[512,256]{1,0:T(8,128)(2,1)S(1)}, u32[]{:S(2)}, u32[]{:S(2)}) collective-permute-start(f16[512,256]{1,0:T(8,128)(2,1)S(1)} %constant_dynamic-update-slice_fusion), channel_id=1, source_target_pairs={{0,4},{1,0},{2,6},{3,2},{4,5},{5,1},{6,7},{7,3},{8,12},{9,8},{10,1... | collective-permute-start | bytes 786440 | tf_op jit(solution)/shard_map/ppermute | solution.py:94
  14.6 2.3 %collective-permute-start.4 = (f32[64,256]{1,0:T(8,128)S(1)}, f32[64,256]{1,0:T(8,128)S(1)}, u32[]{:S(2)}, u32[]{:S(2)}) collective-permute-start(f32[64,256]{1,0:T(8,128)S(1)} %bitcast.3), channel_id=1, source_target_pairs={{0,1},{1,0},{2,3},{3,2},{4,5},{5,4},{6,7},{7,6},{8,9},{9,8},{10,11... | collective-permute-start | bytes 196616 | tf_op jit(solution)/shard_map/ppermute | solution.py:94
  15.1 1.9 %collective-permute-start.5 = (f32[64,256]{1,0:T(8,128)S(1)}, f32[64,256]{1,0:T(8,128)S(1)}, u32[]{:S(2)}, u32[]{:S(2)}) collective-permute-start(f32[64,256]{1,0:T(8,128)S(1)} %collective-permute-done.l2), channel_id=1, source_target_pairs={{0,1},{1,0},{2,3},{3,2},{4,5},{5,4},{6,7},{7,6},{8,9},{9,8},{10,11... | collective-permute-start | bytes 196616 | tf_op jit(solution)/shard_map/ppermute | solution.py:94
  16.4 1.3 %collective-permute-start.8 = (f16[256,256]{1,0:T(8,128)(2,1)S(1)}, f16[256,256]{1,0:T(8,128)(2,1)S(1)}, u32[]{:S(2)}, u32[]{:S(2)}) collective-permute-start(f16[256,256]{1,0:T(8,128)(2,1)S(1)} %collective-permute-done.6), channel_id=1, source_target_pairs={{0,1},{1,0},{2,3},{3,2},{4,5},{5,4},{6,7},{7,6},{8,9},{9,8},{10,11... | collective-permute-start | bytes 393224 | tf_op jit(solution)/shard_map/ppermute | solution.py:94
  16.4 1.5 %collective-permute-start.9 = (f16[256,256]{1,0:T(8,128)(2,1)S(1)}, f16[256,256]{1,0:T(8,128)(2,1)S(1)}, u32[]{:S(2)}, u32[]{:S(2)}) collective-permute-start(f16[256,256]{1,0:T(8,128)(2,1)S(1)} %collective-permute-done.7), channel_id=1, source_target_pairs={{0,1},{1,0},{2,3},{3,2},{4,5},{5,4},{6,7},{7,6},{8,9},{9,8},{10,11... | collective-permute-start | bytes 393224 | tf_op jit(solution)/shard_map/ppermute | solution.py:94
  17.6 1.6 %copy-start = (bf16[2048,512]{1,0:T(8,128)(2,1)S(1)}, bf16[2048,512]{1,0:T(8,128)(2,1)}, u32[]{:S(2)}) copy-start(bf16[2048,512]{1,0:T(8,128)(2,1)} %t_ref.1) | copy-start | bytes 6291460

commit v5 on v4

--- a/solution.py
+++ b/solution.py
@@ -223,12 +223,13 @@
     r = jnp.concatenate([ra, rb], 0)
     xr = send(r, ASIDE)
     inv_y, inv, *_ = barrier((inv_y, inv, r))
-    y0, y1, *_ = barrier((y0, y1, r))
+    y1, *_ = barrier((y1, r))
     inv_k, inv_ky = send(inv, CORE), send(inv_y, CORE)
     ky0, ky1 = send(y0, CORE), send(y1, CORE)
     blocks = (inv, inv_k, inv_y, inv_ky)
     s, hi, lo = early(c, blocks, [widen(v) for v in (p[:NB], p[NB:], m[:NB], m[NB:])])
     sb = late(hi, lo, [widen(v) for v in (y0, y1, ky0, ky1)])
+    xr, _ = barrier((xr, sb))
     sa = s
     here = x == k
     a = jnp.where(here, r[:NB], xr[:NB])

time: 21.3 us -> 21 us (0.986); the launches traced: 21.1 us -> 20.6 us
  local copies, waits for them, and re-layouts: 0.64 us -> 0.21 us
    unnamed x5, local copies, waits for them, and re-layouts: 0.57 us -> 0.13 us
where the time goes in v5:
time: 21 us; the launch traced here: 20.6 us
  starting transfers between devices  9.74 us (46%)
  waiting for transfers between devices  5.83 us (28%)
  Pallas kernels  3.17 us (15%)
  other arithmetic  1.48 us (7%)
  local copies, waits for them, and re-layouts  0.21 us (1%)
    ppermute x11, starting transfers between devices, send(): return lax.ppermute(value, AXES, pairs)  9.74 us
    ppermute x11, waiting for transfers between devices, send(): return lax.ppermute(value, AXES, pairs)  5.83 us
    pallas_call x1, Pallas kernels, final(): pl.pallas_call(final_kernel, out_shape=jax.ShapeDtypeStruct((rows, cols),...  1.96 us
    convert_element_type x2, other arithmetic, narrow(): return (value * SCALE).astype(F16)  1.15 us
    pallas_call x1, Pallas kernels, early(): pl.pallas_call(early_kernel, out_shape=(jax.ShapeDtypeStruct((len(parts),...  0.62 us
    pallas_call x1, Pallas kernels, late(): pl.pallas_call(late_kernel, out_shape=jax.ShapeDtypeStruct((len(parts), n...  0.59 us
  transfers between devices with their start and end apart: 11, of which 4 were waited for; matrix products, arithmetic and copies ran while one was open for 7% of the time, Pallas kernels for 6%

profile of v5, /device:TPU:0, one launch (start us, length us, event | category | flops | bytes accessed | tf_op | source)
XLA Modules:
  0.0 20.6 jit_solution(15359813407379438339)
XLA Ops:
  0.0 0.5 %collective-permute-start.1 = (f32[512,256]{1,0:T(8,128)}, f32[512,256]{1,0:T(8,128)S(1)}, u32[]{:S(2)}, u32[]{:S(2)}) collective-permute-start(f32[512,256]{1,0:T(8,128)} %param.4), channel_id=1, source_target_pairs={{0,1},{1,0},{2,3},{3,2},{4,5},{5,4},{6,7},{7,6},{8,9},{9,8},{10,11... | collective-permute-start | bytes 1572872 | tf_op jit(solution)/shard_map/ppermute | solution.py:94
  0.5 2.5 %collective-permute-start = (f32[64,256]{1,0:T(8,128)}, f32[64,256]{1,0:T(8,128)S(1)}, u32[]{:S(2)}, u32[]{:S(2)}) collective-permute-start(f32[64,256]{1,0:T(8,128)} %bitcast.2), channel_id=1, source_target_pairs={{0,2},{1,3},{2,0},{3,1},{4,6},{5,7},{6,4},{7,5},{8,10},{9,11},{10,... | collective-permute-start | bytes 196616 | tf_op jit(solution)/shard_map/ppermute | solution.py:94
  3.0 1.1 %multiply_convert_fusion.1 = f16[512,256]{1,0:T(8,128)(2,1)S(1)} fusion(f32[512,256]{1,0:T(8,128)} %param.4), kind=kLoop, calls=%fused_computation.1 | loop fusion | flops 262144 | bytes 786432 | tf_op jit(solution)/shard_map/convert_element_type | solution.py:206
  4.1 0.0 copy-start.1
  4.1 0.0 collective-permute-done.1
  4.1 0.1 multiply_convert_fusion
  4.2 3.7 %collective-permute-start.3 = (f16[256,256]{1,0:T(8,128)(2,1)S(1)}, f16[256,256]{1,0:T(8,128)(2,1)S(1)}, u32[]{:S(2)}, u32[]{:S(2)}) collective-permute-start(f16[256,256]{1,0:T(8,128)(2,1)S(1)} %slice_select_fusion), channel_id=1, source_target_pairs={{0,24},{1,0},{2,3},{3,1},{5,29},{4,5},{7,6},{6,4},{8,18},{9,10},{1... | collective-permute-start | bytes 393224 | tf_op jit(solution)/shard_map/ppermute | solution.py:94
  7.9 0.0 collective-permute-start.2
  7.9 0.1 collective-permute-start.7
  8.0 2.0 %collective-permute-start.6 = (f16[256,256]{1,0:T(8,128)(2,1)S(1)}, f16[256,256]{1,0:T(8,128)(2,1)S(1)}, u32[]{:S(2)}, u32[]{:S(2)}) collective-permute-start(f16[256,256]{1,0:T(8,128)(2,1)S(1)} %get-tuple-element.28), channel_id=1, source_target_pairs={{0,2},{1,3},{2,0},{3,1},{4,6},{5,7},{6,4},{7,5},{8,10},{9,11},{10,... | collective-permute-start | bytes 393224 | tf_op jit(solution)/shard_map/ppermute | solution.py:94
  10.0 0.1 convert_multiply_fusion.6
  10.1 4.3 %collective-permute-done.2 = f16[256,256]{1,0:T(8,128)(2,1)S(1)} collective-permute-done((f16[256,256]{1,0:T(8,128)(2,1)S(1)}, f16[256,256]{1,0:T(8,128)(2,1)S(1)}, u32[]{:S(2)}, u32[]{:S(2)}) %collective-permute-start.2) | collective-permute-done | bytes 131104 | tf_op jit(solution)/shard_map/ppermute | solution.py:94
  14.5 0.0 collective-permute-done.3
  14.5 0.0 collective-permute-start.10
  14.6 0.0 collective-permute-done.l2
  14.6 0.5 %collective-permute-start.4 = (f32[64,256]{1,0:T(8,128)S(1)}, f32[64,256]{1,0:T(8,128)S(1)}, u32[]{:S(2)}, u32[]{:S(2)}) collective-permute-start(f32[64,256]{1,0:T(8,128)S(1)} %bitcast.3), channel_id=1, source_target_pairs={{0,1},{1,0},{2,3},{3,2},{4,5},{5,4},{6,7},{7,6},{8,9},{9,8},{10,11... | collective-permute-start | bytes 196616 | tf_op jit(solution)/shard_map/ppermute | solution.py:94
  15.1 0.1 collective-permute-start.5
  15.2 0.0 collective-permute-done.7
  15.2 0.4 %collective-permute-start.9 = (f16[256,256]{1,0:T(8,128)(2,1)S(1)}, f16[256,256]{1,0:T(8,128)(2,1)S(1)}, u32[]{:S(2)}, u32[]{:S(2)}) collective-permute-start(f16[256,256]{1,0:T(8,128)(2,1)S(1)} %collective-permute-done.7), channel_id=1, source_target_pairs={{0,1},{1,0},{2,3},{3,2},{4,5},{5,4},{6,7},{7,6},{8,9},{9,8},{10,11... | collective-permute-start | bytes 393224 | tf_op jit(solution)/shard_map/ppermute | solution.py:94
  15.6 0.8 %collective-permute-done.6 = f16[256,256]{1,0:T(8,128)(2,1)S(1)} collective-permute-done((f16[256,256]{1,0:T(8,128)(2,1)S(1)}, f16[256,256]{1,0:T(8,128)(2,1)S(1)}, u32[]{:S(2)}, u32[]{:S(2)}) %collective-permute-start.6) | collective-permute-done | bytes 131104 | tf_op jit(solution)/shard_map/ppermute | solution.py:94
  16.4 0.0 collective-permute-start.8
  16.4 0.0 collective-permute-done.4.l1
  16.4 0.0 collective-permute-done.5.l3
  16.4 0.6 %shard_map.37 = (bf16[4,256,256]{2,1,0:T(8,128)(2,1)S(1)}, bf16[256,256]{1,0:T(8,128)(2,1)S(1)}, bf16[256,256]{1,0:T(8,128)(2,1)S(1)}) custom-call(s32[1]{0:T(128)} %bitcast.c_ref, f32[64,256]{1,0:T(8,128)S(1)} %bitcast.4, f32[64,256]{1,0:T(8,128)S(1)} %collective-permute-done.4.l1, f32[64,256]{1,0:T(8,128)S(1)} %collective-permute-done.l2, ...), custom_call_target="tpu_custom_call" | custom-call | tf_op jit(solution)/shard_map/pallas_call | solution.py:131
  17.0 0.0 copy-start
  17.1 0.0 collective-permute-done.9
  17.1 0.6 %collective-permute-done.8 = f16[256,256]{1,0:T(8,128)(2,1)S(1)} collective-permute-done((f16[256,256]{1,0:T(8,128)(2,1)S(1)}, f16[256,256]{1,0:T(8,128)(2,1)S(1)}, u32[]{:S(2)}, u32[]{:S(2)}) %collective-permute-start.8) | collective-permute-done | bytes 131104 | tf_op jit(solution)/shard_map/ppermute | solution.py:94
  17.7 0.6 %shard_map.38.sb = bf16[4,256,256]{2,1,0:T(8,128)(2,1)S(1)} custom-call(bf16[256,256]{1,0:T(8,128)(2,1)S(1)} %get-tuple-element.21.hi_ref, bf16[256,256]{1,0:T(8,128)(2,1)S(1)} %get-tuple-element.22.lo_ref, f32[256,256]{1,0:T(8,128)S(1)} %convert_multiply_fusion.5.refs_0_, f32[256,256]{1,0:T(8,128)S(1)} %convert_multiply_fusion.4.refs_1_, ...), custom_call_target="tpu_custom_call" | custom-call | tf_op jit(solution)/shard_map/pallas_call | solution.py:153
  18.3 0.1 collective-permute-done.10
  18.4 0.1 convert_multiply_fusion
  18.5 0.1 copy-done
  18.6 2.0 %shard_map.39 = bf16[2048,512]{1,0:T(8,128)(2,1)} custom-call(s32[1]{0:T(128)} %bitcast.c_ref, bf16[2048,512]{1,0:T(8,128)(2,1)S(1)} %copy-done, bf16[4,256,256]{2,1,0:T(8,128)(2,1)S(1)} %get-tuple-element.20.sa, bf16[4,256,256]{2,1,0:T(8,128)(2,1)S(1)} %shard_map.38.sb, f32[256,256]{1,0:T(8,128)S(1)} %get-tuple-element.26.ta, ...), custom_call_target="tpu_custom_call" | custom-call | tf_op jit(solution)/shard_map/pallas_call | solution.py:187
  (9 shorter events, 0.2 us)
Async XLA Ops:
  0.0 4.1 %collective-permute-start.1 = (f32[512,256]{1,0:T(8,128)}, f32[512,256]{1,0:T(8,128)S(1)}, u32[]{:S(2)}, u32[]{:S(2)}) collective-permute-start(f32[512,256]{1,0:T(8,128)} %param.4), channel_id=1, source_target_pairs={{0,1},{1,0},{2,3},{3,2},{4,5},{5,4},{6,7},{7,6},{8,9},{9,8},{10,11... | collective-permute-start | bytes 1572872 | tf_op jit(solution)/shard_map/ppermute | solution.py:94
  0.5 14.1 %collective-permute-start = (f32[64,256]{1,0:T(8,128)}, f32[64,256]{1,0:T(8,128)S(1)}, u32[]{:S(2)}, u32[]{:S(2)}) collective-permute-start(f32[64,256]{1,0:T(8,128)} %bitcast.2), channel_id=1, source_target_pairs={{0,2},{1,3},{2,0},{3,1},{4,6},{5,7},{6,4},{7,5},{8,10},{9,11},{10,... | collective-permute-start | bytes 196616 | tf_op jit(solution)/shard_map/ppermute | solution.py:94
  4.1 10.5 %copy-start.1 = (f32[256,64]{0,1:T(8,128)S(1)}, f32[256,64]{0,1:T(8,128)}, u32[]{:S(2)}) copy-start(f32[256,64]{0,1:T(8,128)} %param.5) | copy-start | bytes 196612
  4.2 10.3 %collective-permute-start.3 = (f16[256,256]{1,0:T(8,128)(2,1)S(1)}, f16[256,256]{1,0:T(8,128)(2,1)S(1)}, u32[]{:S(2)}, u32[]{:S(2)}) collective-permute-start(f16[256,256]{1,0:T(8,128)(2,1)S(1)} %slice_select_fusion), channel_id=1, source_target_pairs={{0,24},{1,0},{2,3},{3,1},{5,29},{4,5},{7,6},{6,4},{8,18},{9,10},{1... | collective-permute-start | bytes 393224 | tf_op jit(solution)/shard_map/ppermute | solution.py:94
  7.9 6.6 %collective-permute-start.2 = (f16[256,256]{1,0:T(8,128)(2,1)S(1)}, f16[256,256]{1,0:T(8,128)(2,1)S(1)}, u32[]{:S(2)}, u32[]{:S(2)}) collective-permute-start(f16[256,256]{1,0:T(8,128)(2,1)S(1)} %slice_select_fusion), channel_id=1, source_target_pairs={{0,8},{1,16},{2,3},{3,1},{5,13},{4,21},{7,6},{6,4},{8,2},{9,26},{1... | collective-permute-start | bytes 393224 | tf_op jit(solution)/shard_map/ppermute | solution.py:94
  7.9 7.2 %collective-permute-start.7 = (f16[256,256]{1,0:T(8,128)(2,1)S(1)}, f16[256,256]{1,0:T(8,128)(2,1)S(1)}, u32[]{:S(2)}, u32[]{:S(2)}) collective-permute-start(f16[256,256]{1,0:T(8,128)(2,1)S(1)} %get-tuple-element.27), channel_id=1, source_target_pairs={{0,2},{1,3},{2,0},{3,1},{4,6},{5,7},{6,4},{7,5},{8,10},{9,11},{10,... | collective-permute-start | bytes 393224 | tf_op jit(solution)/shard_map/ppermute | solution.py:94
  8.0 8.4 %collective-permute-start.6 = (f16[256,256]{1,0:T(8,128)(2,1)S(1)}, f16[256,256]{1,0:T(8,128)(2,1)S(1)}, u32[]{:S(2)}, u32[]{:S(2)}) collective-permute-start(f16[256,256]{1,0:T(8,128)(2,1)S(1)} %get-tuple-element.28), channel_id=1, source_target_pairs={{0,2},{1,3},{2,0},{3,1},{4,6},{5,7},{6,4},{7,5},{8,10},{9,11},{10,... | collective-permute-start | bytes 393224 | tf_op jit(solution)/shard_map/ppermute | solution.py:94
  14.5 3.9 %collective-permute-start.10 = (f16[512,256]{1,0:T(8,128)(2,1)S(1)}, f16[512,256]{1,0:T(8,128)(2,1)S(1)}, u32[]{:S(2)}, u32[]{:S(2)}) collective-permute-start(f16[512,256]{1,0:T(8,128)(2,1)S(1)} %constant_dynamic-update-slice_fusion), channel_id=1, source_target_pairs={{0,4},{1,0},{2,6},{3,2},{4,5},{5,1},{6,7},{7,3},{8,12},{9,8},{10,1... | collective-permute-start | bytes 786440 | tf_op jit(solution)/shard_map/ppermute | solution.py:94
  14.6 1.8 %collective-permute-start.4 = (f32[64,256]{1,0:T(8,128)S(1)}, f32[64,256]{1,0:T(8,128)S(1)}, u32[]{:S(2)}, u32[]{:S(2)}) collective-permute-start(f32[64,256]{1,0:T(8,128)S(1)} %bitcast.3), channel_id=1, source_target_pairs={{0,1},{1,0},{2,3},{3,2},{4,5},{5,4},{6,7},{7,6},{8,9},{9,8},{10,11... | collective-permute-start | bytes 196616 | tf_op jit(solution)/shard_map/ppermute | solution.py:94
  15.1 1.3 %collective-permute-start.5 = (f32[64,256]{1,0:T(8,128)S(1)}, f32[64,256]{1,0:T(8,128)S(1)}, u32[]{:S(2)}, u32[]{:S(2)}) collective-permute-start(f32[64,256]{1,0:T(8,128)S(1)} %collective-permute-done.l2), channel_id=1, source_target_pairs={{0,1},{1,0},{2,3},{3,2},{4,5},{5,4},{6,7},{7,6},{8,9},{9,8},{10,11... | collective-permute-start | bytes 196616 | tf_op jit(solution)/shard_map/ppermute | solution.py:94
  15.2 1.9 %collective-permute-start.9 = (f16[256,256]{1,0:T(8,128)(2,1)S(1)}, f16[256,256]{1,0:T(8,128)(2,1)S(1)}, u32[]{:S(2)}, u32[]{:S(2)}) collective-permute-start(f16[256,256]{1,0:T(8,128)(2,1)S(1)} %collective-permute-done.7), channel_id=1, source_target_pairs={{0,1},{1,0},{2,3},{3,2},{4,5},{5,4},{6,7},{7,6},{8,9},{9,8},{10,11... | collective-permute-start | bytes 393224 | tf_op jit(solution)/shard_map/ppermute | solution.py:94
  16.4 1.3 %collective-permute-start.8 = (f16[256,256]{1,0:T(8,128)(2,1)S(1)}, f16[256,256]{1,0:T(8,128)(2,1)S(1)}, u32[]{:S(2)}, u32[]{:S(2)}) collective-permute-start(f16[256,256]{1,0:T(8,128)(2,1)S(1)} %collective-permute-done.6), channel_id=1, source_target_pairs={{0,1},{1,0},{2,3},{3,2},{4,5},{5,4},{6,7},{7,6},{8,9},{9,8},{10,11... | collective-permute-start | bytes 393224 | tf_op jit(solution)/shard_map/ppermute | solution.py:94
  17.0 1.6 %copy-start = (bf16[2048,512]{1,0:T(8,128)(2,1)S(1)}, bf16[2048,512]{1,0:T(8,128)(2,1)}, u32[]{:S(2)}) copy-start(bf16[2048,512]{1,0:T(8,128)(2,1)} %t_ref.1) | copy-start | bytes 6291460

commit v6 on v5

--- a/solution.py
+++ b/solution.py
@@ -108,7 +108,7 @@
     return (mul(hi, lt_hi) + (mul(hi, lt_lo) + mul(lo, lt_hi))).astype(BF16)
 
 
-def early_kernel(c_ref, l0, l1, l2, l3, *refs):
+def early_kernel(c_ref, _, l0, l1, l2, l3, *refs):
     s_ref, hi_ref, lo_ref, lt_ref = refs[-4:]
     c = c_ref[0]
     for i, block in enumerate((l0, l1, l2, l3)):
@@ -126,7 +126,7 @@
 LIMIT = pltpu.CompilerParams(vmem_limit_bytes=24 * 1024 * 1024)
 
 
-def early(c, blocks, parts):
+def early(c, trailing, blocks, parts):
     n = parts[0].shape[0]
     return pl.pallas_call(
         early_kernel,
@@ -135,11 +135,11 @@
             jax.ShapeDtypeStruct((NB, NB), BF16),
             jax.ShapeDtypeStruct((NB, NB), BF16),
         ),
-        in_specs=[SMEM] + [VMEM] * (4 + len(parts)),
+        in_specs=[SMEM, VMEM] + [VMEM] * (4 + len(parts)),
         out_specs=(VMEM, VMEM, VMEM),
         scratch_shapes=[pltpu.VMEM((NB, NB), F32)],
         compiler_params=LIMIT,
-    )(c, *blocks, *parts)
+    )(c, trailing, *blocks, *parts)
 
 
 def late_kernel(hi_ref, lo_ref, *refs):
@@ -227,7 +227,7 @@
     inv_k, inv_ky = send(inv, CORE), send(inv_y, CORE)
     ky0, ky1 = send(y0, CORE), send(y1, CORE)
     blocks = (inv, inv_k, inv_y, inv_ky)
-    s, hi, lo = early(c, blocks, [widen(v) for v in (p[:NB], p[NB:], m[:NB], m[NB:])])
+    s, hi, lo = early(c, trailing, blocks, [widen(v) for v in (p[:NB], p[NB:], m[:NB], m[NB:])])
     sb = late(hi, lo, [widen(v) for v in (y0, y1, ky0, ky1)])
     xr, _ = barrier((xr, sb))
     sa = s

time: 21 us -> 20.7 us (0.986); the launches traced: 20.6 us -> 20.5 us
  no operation moved by 1% of the time
where the time goes in v6:
time: 20.7 us; the launch traced here: 20.5 us
  starting transfers between devices  9.74 us (47%)
  waiting for transfers between devices  5.85 us (28%)
  Pallas kernels  3.17 us (15%)
  other arithmetic  1.48 us (7%)
    ppermute x11, starting transfers between devices, send(): return lax.ppermute(value, AXES, pairs)  9.74 us
    ppermute x11, waiting for transfers between devices, send(): return lax.ppermute(value, AXES, pairs)  5.85 us
    pallas_call x1, Pallas kernels, final(): pl.pallas_call(final_kernel, out_shape=jax.ShapeDtypeStruct((rows, cols),...  1.98 us
    convert_element_type x2, other arithmetic, narrow(): return (value * SCALE).astype(F16)  1.15 us
    pallas_call x1, Pallas kernels, early(): pl.pallas_call(early_kernel, out_shape=(jax.ShapeDtypeStruct((len(parts),...  0.62 us
    pallas_call x1, Pallas kernels, late(): pl.pallas_call(late_kernel, out_shape=jax.ShapeDtypeStruct((len(parts), n...  0.58 us
  transfers between devices with their start and end apart: 11, of which 4 were waited for; matrix products, arithmetic and copies ran while one was open for 7% of the time, Pallas kernels for 6%

profile of v6, /device:TPU:0, one launch (start us, length us, event | category | flops | bytes accessed | tf_op | source)
XLA Modules:
  0.0 20.5 jit_solution(12535370765948874719)
XLA Ops:
  0.0 0.5 %collective-permute-start.1 = (f32[512,256]{1,0:T(8,128)}, f32[512,256]{1,0:T(8,128)S(1)}, u32[]{:S(2)}, u32[]{:S(2)}) collective-permute-start(f32[512,256]{1,0:T(8,128)} %param.4), channel_id=1, source_target_pairs={{0,1},{1,0},{2,3},{3,2},{4,5},{5,4},{6,7},{7,6},{8,9},{9,8},{10,11... | collective-permute-start | bytes 1572872 | tf_op jit(solution)/shard_map/ppermute | solution.py:94
  0.5 2.5 %collective-permute-start = (f32[64,256]{1,0:T(8,128)}, f32[64,256]{1,0:T(8,128)S(1)}, u32[]{:S(2)}, u32[]{:S(2)}) collective-permute-start(f32[64,256]{1,0:T(8,128)} %bitcast.2), channel_id=1, source_target_pairs={{0,2},{1,3},{2,0},{3,1},{4,6},{5,7},{6,4},{7,5},{8,10},{9,11},{10,... | collective-permute-start | bytes 196616 | tf_op jit(solution)/shard_map/ppermute | solution.py:94
  3.0 1.1 %multiply_convert_fusion.1 = f16[512,256]{1,0:T(8,128)(2,1)S(1)} fusion(f32[512,256]{1,0:T(8,128)} %param.4), kind=kLoop, calls=%fused_computation.1 | loop fusion | flops 262144 | bytes 786432 | tf_op jit(solution)/shard_map/convert_element_type | solution.py:206
  4.1 0.0 copy-start.1
  4.1 0.0 collective-permute-done.1
  4.1 0.1 multiply_convert_fusion
  4.2 0.0 copy-start
  4.2 3.7 %collective-permute-start.3 = (f16[256,256]{1,0:T(8,128)(2,1)S(1)}, f16[256,256]{1,0:T(8,128)(2,1)S(1)}, u32[]{:S(2)}, u32[]{:S(2)}) collective-permute-start(f16[256,256]{1,0:T(8,128)(2,1)S(1)} %slice_select_fusion), channel_id=1, source_target_pairs={{0,24},{1,0},{2,3},{3,1},{5,29},{4,5},{7,6},{6,4},{8,18},{9,10},{1... | collective-permute-start | bytes 393224 | tf_op jit(solution)/shard_map/ppermute | solution.py:94
  7.9 0.0 collective-permute-start.2
  7.9 0.1 collective-permute-start.7
  8.0 2.0 %collective-permute-start.6 = (f16[256,256]{1,0:T(8,128)(2,1)S(1)}, f16[256,256]{1,0:T(8,128)(2,1)S(1)}, u32[]{:S(2)}, u32[]{:S(2)}) collective-permute-start(f16[256,256]{1,0:T(8,128)(2,1)S(1)} %get-tuple-element.28), channel_id=1, source_target_pairs={{0,2},{1,3},{2,0},{3,1},{4,6},{5,7},{6,4},{7,5},{8,10},{9,11},{10,... | collective-permute-start | bytes 393224 | tf_op jit(solution)/shard_map/ppermute | solution.py:94
  10.0 0.1 convert_multiply_fusion.6
  10.1 4.3 %collective-permute-done.2 = f16[256,256]{1,0:T(8,128)(2,1)S(1)} collective-permute-done((f16[256,256]{1,0:T(8,128)(2,1)S(1)}, f16[256,256]{1,0:T(8,128)(2,1)S(1)}, u32[]{:S(2)}, u32[]{:S(2)}) %collective-permute-start.2) | collective-permute-done | bytes 131104 | tf_op jit(solution)/shard_map/ppermute | solution.py:94
  14.5 0.0 collective-permute-done.3
  14.5 0.0 collective-permute-start.10
  14.6 0.0 collective-permute-done.l2
  14.6 0.0 copy-done.1
  14.6 0.5 %collective-permute-start.4 = (f32[64,256]{1,0:T(8,128)S(1)}, f32[64,256]{1,0:T(8,128)S(1)}, u32[]{:S(2)}, u32[]{:S(2)}) collective-permute-start(f32[64,256]{1,0:T(8,128)S(1)} %bitcast.3), channel_id=1, source_target_pairs={{0,1},{1,0},{2,3},{3,2},{4,5},{5,4},{6,7},{7,6},{8,9},{9,8},{10,11... | collective-permute-start | bytes 196616 | tf_op jit(solution)/shard_map/ppermute | solution.py:94
  15.1 0.1 collective-permute-start.5
  15.2 0.0 collective-permute-done.7
  15.2 0.4 %collective-permute-start.9 = (f16[256,256]{1,0:T(8,128)(2,1)S(1)}, f16[256,256]{1,0:T(8,128)(2,1)S(1)}, u32[]{:S(2)}, u32[]{:S(2)}) collective-permute-start(f16[256,256]{1,0:T(8,128)(2,1)S(1)} %collective-permute-done.7), channel_id=1, source_target_pairs={{0,1},{1,0},{2,3},{3,2},{4,5},{5,4},{6,7},{7,6},{8,9},{9,8},{10,11... | collective-permute-start | bytes 393224 | tf_op jit(solution)/shard_map/ppermute | solution.py:94
  15.6 0.8 %collective-permute-done.6 = f16[256,256]{1,0:T(8,128)(2,1)S(1)} collective-permute-done((f16[256,256]{1,0:T(8,128)(2,1)S(1)}, f16[256,256]{1,0:T(8,128)(2,1)S(1)}, u32[]{:S(2)}, u32[]{:S(2)}) %collective-permute-start.6) | collective-permute-done | bytes 131104 | tf_op jit(solution)/shard_map/ppermute | solution.py:94
  16.4 0.0 collective-permute-start.8
  16.4 0.0 collective-permute-done.4.l1
  16.4 0.0 collective-permute-done.5.l3
  16.4 0.6 %shard_map.37 = (bf16[4,256,256]{2,1,0:T(8,128)(2,1)S(1)}, bf16[256,256]{1,0:T(8,128)(2,1)S(1)}, bf16[256,256]{1,0:T(8,128)(2,1)S(1)}) custom-call(s32[1]{0:T(128)} %bitcast.c_ref, bf16[2048,512]{1,0:T(8,128)(2,1)S(1)} %copy-done, f32[64,256]{1,0:T(8,128)S(1)} %bitcast.4, f32[64,256]{1,0:T(8,128)S(1)} %collective-permute-done.4.l1, ...), custom_call_target="tpu_custom_call" | custom-call | tf_op jit(solution)/shard_map/pallas_call | solution.py:131
  17.1 0.0 collective-permute-done.9
  17.1 0.6 %collective-permute-done.8 = f16[256,256]{1,0:T(8,128)(2,1)S(1)} collective-permute-done((f16[256,256]{1,0:T(8,128)(2,1)S(1)}, f16[256,256]{1,0:T(8,128)(2,1)S(1)}, u32[]{:S(2)}, u32[]{:S(2)}) %collective-permute-start.8) | collective-permute-done | bytes 131104 | tf_op jit(solution)/shard_map/ppermute | solution.py:94
  17.8 0.6 %shard_map.38.sb = bf16[4,256,256]{2,1,0:T(8,128)(2,1)S(1)} custom-call(bf16[256,256]{1,0:T(8,128)(2,1)S(1)} %get-tuple-element.21.hi_ref, bf16[256,256]{1,0:T(8,128)(2,1)S(1)} %get-tuple-element.22.lo_ref, f32[256,256]{1,0:T(8,128)S(1)} %convert_multiply_fusion.5.refs_0_, f32[256,256]{1,0:T(8,128)S(1)} %convert_multiply_fusion.4.refs_1_, ...), custom_call_target="tpu_custom_call" | custom-call | tf_op jit(solution)/shard_map/pallas_call | solution.py:153
  18.3 0.1 collective-permute-done.10
  18.5 0.1 convert_multiply_fusion
  18.5 2.0 %shard_map.39 = bf16[2048,512]{1,0:T(8,128)(2,1)} custom-call(s32[1]{0:T(128)} %bitcast.c_ref, bf16[2048,512]{1,0:T(8,128)(2,1)S(1)} %copy-done, bf16[4,256,256]{2,1,0:T(8,128)(2,1)S(1)} %get-tuple-element.20.sa, bf16[4,256,256]{2,1,0:T(8,128)(2,1)S(1)} %shard_map.38.sb, f32[256,256]{1,0:T(8,128)S(1)} %get-tuple-element.26.ta, ...), custom_call_target="tpu_custom_call" | custom-call | tf_op jit(solution)/shard_map/pallas_call | solution.py:187
  (9 shorter events, 0.2 us)
Async XLA Ops:
  0.0 4.1 %collective-permute-start.1 = (f32[512,256]{1,0:T(8,128)}, f32[512,256]{1,0:T(8,128)S(1)}, u32[]{:S(2)}, u32[]{:S(2)}) collective-permute-start(f32[512,256]{1,0:T(8,128)} %param.4), channel_id=1, source_target_pairs={{0,1},{1,0},{2,3},{3,2},{4,5},{5,4},{6,7},{7,6},{8,9},{9,8},{10,11... | collective-permute-start | bytes 1572872 | tf_op jit(solution)/shard_map/ppermute | solution.py:94
  0.5 14.1 %collective-permute-start = (f32[64,256]{1,0:T(8,128)}, f32[64,256]{1,0:T(8,128)S(1)}, u32[]{:S(2)}, u32[]{:S(2)}) collective-permute-start(f32[64,256]{1,0:T(8,128)} %bitcast.2), channel_id=1, source_target_pairs={{0,2},{1,3},{2,0},{3,1},{4,6},{5,7},{6,4},{7,5},{8,10},{9,11},{10,... | collective-permute-start | bytes 196616 | tf_op jit(solution)/shard_map/ppermute | solution.py:94
  4.1 10.5 %copy-start.1 = (f32[256,64]{0,1:T(8,128)S(1)}, f32[256,64]{0,1:T(8,128)}, u32[]{:S(2)}) copy-start(f32[256,64]{0,1:T(8,128)} %param.5) | copy-start | bytes 196612
  4.2 12.3 %copy-start = (bf16[2048,512]{1,0:T(8,128)(2,1)S(1)}, bf16[2048,512]{1,0:T(8,128)(2,1)}, u32[]{:S(2)}) copy-start(bf16[2048,512]{1,0:T(8,128)(2,1)} %t_ref.1) | copy-start | bytes 6291460
  4.2 10.3 %collective-permute-start.3 = (f16[256,256]{1,0:T(8,128)(2,1)S(1)}, f16[256,256]{1,0:T(8,128)(2,1)S(1)}, u32[]{:S(2)}, u32[]{:S(2)}) collective-permute-start(f16[256,256]{1,0:T(8,128)(2,1)S(1)} %slice_select_fusion), channel_id=1, source_target_pairs={{0,24},{1,0},{2,3},{3,1},{5,29},{4,5},{7,6},{6,4},{8,18},{9,10},{1... | collective-permute-start | bytes 393224 | tf_op jit(solution)/shard_map/ppermute | solution.py:94
  7.9 6.6 %collective-permute-start.2 = (f16[256,256]{1,0:T(8,128)(2,1)S(1)}, f16[256,256]{1,0:T(8,128)(2,1)S(1)}, u32[]{:S(2)}, u32[]{:S(2)}) collective-permute-start(f16[256,256]{1,0:T(8,128)(2,1)S(1)} %slice_select_fusion), channel_id=1, source_target_pairs={{0,8},{1,16},{2,3},{3,1},{5,13},{4,21},{7,6},{6,4},{8,2},{9,26},{1... | collective-permute-start | bytes 393224 | tf_op jit(solution)/shard_map/ppermute | solution.py:94
  7.9 7.2 %collective-permute-start.7 = (f16[256,256]{1,0:T(8,128)(2,1)S(1)}, f16[256,256]{1,0:T(8,128)(2,1)S(1)}, u32[]{:S(2)}, u32[]{:S(2)}) collective-permute-start(f16[256,256]{1,0:T(8,128)(2,1)S(1)} %get-tuple-element.27), channel_id=1, source_target_pairs={{0,2},{1,3},{2,0},{3,1},{4,6},{5,7},{6,4},{7,5},{8,10},{9,11},{10,... | collective-permute-start | bytes 393224 | tf_op jit(solution)/shard_map/ppermute | solution.py:94
  8.0 8.4 %collective-permute-start.6 = (f16[256,256]{1,0:T(8,128)(2,1)S(1)}, f16[256,256]{1,0:T(8,128)(2,1)S(1)}, u32[]{:S(2)}, u32[]{:S(2)}) collective-permute-start(f16[256,256]{1,0:T(8,128)(2,1)S(1)} %get-tuple-element.28), channel_id=1, source_target_pairs={{0,2},{1,3},{2,0},{3,1},{4,6},{5,7},{6,4},{7,5},{8,10},{9,11},{10,... | collective-permute-start | bytes 393224 | tf_op jit(solution)/shard_map/ppermute | solution.py:94
  14.5 3.9 %collective-permute-start.10 = (f16[512,256]{1,0:T(8,128)(2,1)S(1)}, f16[512,256]{1,0:T(8,128)(2,1)S(1)}, u32[]{:S(2)}, u32[]{:S(2)}) collective-permute-start(f16[512,256]{1,0:T(8,128)(2,1)S(1)} %constant_dynamic-update-slice_fusion), channel_id=1, source_target_pairs={{0,4},{1,0},{2,6},{3,2},{4,5},{5,1},{6,7},{7,3},{8,12},{9,8},{10,1... | collective-permute-start | bytes 786440 | tf_op jit(solution)/shard_map/ppermute | solution.py:94
  14.6 1.8 %collective-permute-start.4 = (f32[64,256]{1,0:T(8,128)S(1)}, f32[64,256]{1,0:T(8,128)S(1)}, u32[]{:S(2)}, u32[]{:S(2)}) collective-permute-start(f32[64,256]{1,0:T(8,128)S(1)} %bitcast.3), channel_id=1, source_target_pairs={{0,1},{1,0},{2,3},{3,2},{4,5},{5,4},{6,7},{7,6},{8,9},{9,8},{10,11... | collective-permute-start | bytes 196616 | tf_op jit(solution)/shard_map/ppermute | solution.py:94
  15.1 1.3 %collective-permute-start.5 = (f32[64,256]{1,0:T(8,128)S(1)}, f32[64,256]{1,0:T(8,128)S(1)}, u32[]{:S(2)}, u32[]{:S(2)}) collective-permute-start(f32[64,256]{1,0:T(8,128)S(1)} %collective-permute-done.l2), channel_id=1, source_target_pairs={{0,1},{1,0},{2,3},{3,2},{4,5},{5,4},{6,7},{7,6},{8,9},{9,8},{10,11... | collective-permute-start | bytes 196616 | tf_op jit(solution)/shard_map/ppermute | solution.py:94
  15.2 1.9 %collective-permute-start.9 = (f16[256,256]{1,0:T(8,128)(2,1)S(1)}, f16[256,256]{1,0:T(8,128)(2,1)S(1)}, u32[]{:S(2)}, u32[]{:S(2)}) collective-permute-start(f16[256,256]{1,0:T(8,128)(2,1)S(1)} %collective-permute-done.7), channel_id=1, source_target_pairs={{0,1},{1,0},{2,3},{3,2},{4,5},{5,4},{6,7},{7,6},{8,9},{9,8},{10,11... | collective-permute-start | bytes 393224 | tf_op jit(solution)/shard_map/ppermute | solution.py:94
  16.4 1.3 %collective-permute-start.8 = (f16[256,256]{1,0:T(8,128)(2,1)S(1)}, f16[256,256]{1,0:T(8,128)(2,1)S(1)}, u32[]{:S(2)}, u32[]{:S(2)}) collective-permute-start(f16[256,256]{1,0:T(8,128)(2,1)S(1)} %collective-permute-done.6), channel_id=1, source_target_pairs={{0,1},{1,0},{2,3},{3,2},{4,5},{5,4},{6,7},{7,6},{8,9},{9,8},{10,11... | collective-permute-start | bytes 393224 | tf_op jit(solution)/shard_map/ppermute | solution.py:94

commit v7 on v6

--- a/solution.py
+++ b/solution.py
@@ -10,7 +10,7 @@
 SCALE = 32768.0
 ORDER = (
     ((0, 0), 0, 0), ((0, 1), 0, 1), ((0, 2), 1, 0), ((0, 3), 1, 1),
-    ((1, 0), 2, 0), ((1, 1), 2, 1), ((1, 2), 3, 0), ((1, 3), 3, 1),
+    ((1, 0), 2, 0), ((1, 1), 3, 0), ((2, 0), 2, 1), ((2, 1), 3, 1),
 )
 AXES = ("row", "col")
 F32, F16, BF16 = jnp.float32, jnp.float16, jnp.bfloat16
@@ -159,7 +159,7 @@
     )(hi, lo, *parts)
 
 
-def final_kernel(c_ref, t_ref, sa, sb, ta, tb, hi_ref, lo_ref, o_ref, m_ref, buf, sems):
+def final_kernel(c_ref, t_ref, sa, sb, sc, ta, tb, hi_ref, lo_ref, o_ref, m_ref, buf, sems):
     c = c_ref[0]
     n = buf.shape[1]
     hi, lo = hi_ref[...], lo_ref[...]
@@ -169,7 +169,7 @@
     copies = []
     for i, (source, part, row) in enumerate(ORDER):
         at = pl.multiple_of((c ^ part) * 2 * n + row * n, n)
-        rows = (sa, sb)[source[0]][source[1]]
+        rows = (sa, sb, sc)[source[0]][source[1]]
         update = lax.dot_general(
             rows, mirror, (((1,), (1,)), ((), ())), preferred_element_type=F32
         )
@@ -181,13 +181,13 @@
         copy.wait()
 
 
-def final(c, trailing, sa, sb, ta, tb, hi, lo):
+def final(c, trailing, sa, sb, sc, ta, tb, hi, lo):
     rows, cols = trailing.shape
     n = rows // 8
     return pl.pallas_call(
         final_kernel,
         out_shape=jax.ShapeDtypeStruct((rows, cols), BF16),
-        in_specs=[SMEM] + [VMEM] * 7,
+        in_specs=[SMEM] + [VMEM] * 8,
         out_specs=pl.BlockSpec(memory_space=pl.ANY),
         scratch_shapes=[
             pltpu.VMEM((2 * NB, NB), BF16),
@@ -195,7 +195,7 @@
             pltpu.SemaphoreType.DMA((8,)),
         ],
         compiler_params=LIMIT,
-    )(c, trailing, sa, sb, ta, tb, hi, lo)
+    )(c, trailing, sa, sb, sc, ta, tb, hi, lo)
 
 
 def widen(value):
@@ -228,8 +228,9 @@
     ky0, ky1 = send(y0, CORE), send(y1, CORE)
     blocks = (inv, inv_k, inv_y, inv_ky)
     s, hi, lo = early(c, trailing, blocks, [widen(v) for v in (p[:NB], p[NB:], m[:NB], m[NB:])])
-    sb = late(hi, lo, [widen(v) for v in (y0, y1, ky0, ky1)])
-    xr, _ = barrier((xr, sb))
+    sb = late(hi, lo, [widen(v) for v in (y0, ky0)])
+    sc = late(hi, lo, [widen(v) for v in (y1, ky1)])
+    xr, _ = barrier((xr, sc))
     sa = s
     here = x == k
     a = jnp.where(here, r[:NB], xr[:NB])
@@ -237,7 +238,7 @@
     a_low = jnp.where(z % 2 == y, z >= 2, z < 2)
     ta = widen(jnp.where(a_low, a, b))
     tb = widen(jnp.where(a_low, b, a))
-    return final(c, trailing, sa, sb, ta, tb, hi, lo)
+    return final(c, trailing, sa, sb, sc, ta, tb, hi, lo)
 
 
 def solution(mesh):

time: 20.7 us -> 20.7 us (level)
    pallas_call x1 -> x2, Pallas kernels: 0.58 us -> 0.76 us  [late(): pl.pallas_call(late_kernel, out_shape=jax.ShapeDtypeStruct((len(parts), n...]
  transfers between devices with their start and end apart: 11 -> 11, of which waited for: 4 -> 4; matrix products, arithmetic and copies ran while one was open for 7% -> 7% of each run, Pallas kernels for 6% -> 7%
where the time goes in v7:
time: 20.7 us; the launch traced here: 20.5 us
  starting transfers between devices  9.74 us (47%)
  waiting for transfers between devices  5.65 us (27%)
  Pallas kernels  3.35 us (16%)
  other arithmetic  1.48 us (7%)
    ppermute x11, starting transfers between devices, send(): return lax.ppermute(value, AXES, pairs)  9.74 us
    ppermute x11, waiting for transfers between devices, send(): return lax.ppermute(value, AXES, pairs)  5.65 us
    pallas_call x1, Pallas kernels, final(): pl.pallas_call(final_kernel, out_shape=jax.ShapeDtypeStruct((rows, cols),...  1.98 us
    convert_element_type x2, other arithmetic, narrow(): return (value * SCALE).astype(F16)  1.15 us
    pallas_call x2, Pallas kernels, late(): pl.pallas_call(late_kernel, out_shape=jax.ShapeDtypeStruct((len(parts), n...  0.76 us
    pallas_call x1, Pallas kernels, early(): pl.pallas_call(early_kernel, out_shape=(jax.ShapeDtypeStruct((len(parts),...  0.62 us
  transfers between devices with their start and end apart: 11, of which 4 were waited for; matrix products, arithmetic and copies ran while one was open for 7% of the time, Pallas kernels for 7%

profile of v7, /device:TPU:0, one launch (start us, length us, event | category | flops | bytes accessed | tf_op | source)
XLA Modules:
  0.0 20.5 jit_solution(6516321835872965685)
XLA Ops:
  0.0 0.5 %collective-permute-start.1 = (f32[512,256]{1,0:T(8,128)}, f32[512,256]{1,0:T(8,128)S(1)}, u32[]{:S(2)}, u32[]{:S(2)}) collective-permute-start(f32[512,256]{1,0:T(8,128)} %param.4), channel_id=1, source_target_pairs={{0,1},{1,0},{2,3},{3,2},{4,5},{5,4},{6,7},{7,6},{8,9},{9,8},{10,11... | collective-permute-start | bytes 1572872 | tf_op jit(solution)/shard_map/ppermute | solution.py:94
  0.5 2.5 %collective-permute-start = (f32[64,256]{1,0:T(8,128)}, f32[64,256]{1,0:T(8,128)S(1)}, u32[]{:S(2)}, u32[]{:S(2)}) collective-permute-start(f32[64,256]{1,0:T(8,128)} %bitcast.2), channel_id=1, source_target_pairs={{0,2},{1,3},{2,0},{3,1},{4,6},{5,7},{6,4},{7,5},{8,10},{9,11},{10,... | collective-permute-start | bytes 196616 | tf_op jit(solution)/shard_map/ppermute | solution.py:94
  3.0 1.1 %multiply_convert_fusion.1 = f16[512,256]{1,0:T(8,128)(2,1)S(1)} fusion(f32[512,256]{1,0:T(8,128)} %param.4), kind=kLoop, calls=%fused_computation.1 | loop fusion | flops 262144 | bytes 786432 | tf_op jit(solution)/shard_map/convert_element_type | solution.py:206
  4.1 0.0 copy-start.1
  4.1 0.0 collective-permute-done.1
  4.1 0.1 multiply_convert_fusion
  4.2 0.0 copy-start
  4.2 3.7 %collective-permute-start.3 = (f16[256,256]{1,0:T(8,128)(2,1)S(1)}, f16[256,256]{1,0:T(8,128)(2,1)S(1)}, u32[]{:S(2)}, u32[]{:S(2)}) collective-permute-start(f16[256,256]{1,0:T(8,128)(2,1)S(1)} %slice_select_fusion), channel_id=1, source_target_pairs={{0,24},{1,0},{2,3},{3,1},{5,29},{4,5},{7,6},{6,4},{8,18},{9,10},{1... | collective-permute-start | bytes 393224 | tf_op jit(solution)/shard_map/ppermute | solution.py:94
  7.9 0.0 collective-permute-start.2
  7.9 0.1 collective-permute-start.8
  8.0 2.0 %collective-permute-start.6 = (f16[256,256]{1,0:T(8,128)(2,1)S(1)}, f16[256,256]{1,0:T(8,128)(2,1)S(1)}, u32[]{:S(2)}, u32[]{:S(2)}) collective-permute-start(f16[256,256]{1,0:T(8,128)(2,1)S(1)} %get-tuple-element.28), channel_id=1, source_target_pairs={{0,2},{1,3},{2,0},{3,1},{4,6},{5,7},{6,4},{7,5},{8,10},{9,11},{10,... | collective-permute-start | bytes 393224 | tf_op jit(solution)/shard_map/ppermute | solution.py:94
  10.0 0.1 convert_multiply_fusion.6
  10.1 4.3 %collective-permute-done.2 = f16[256,256]{1,0:T(8,128)(2,1)S(1)} collective-permute-done((f16[256,256]{1,0:T(8,128)(2,1)S(1)}, f16[256,256]{1,0:T(8,128)(2,1)S(1)}, u32[]{:S(2)}, u32[]{:S(2)}) %collective-permute-start.2) | collective-permute-done | bytes 131104 | tf_op jit(solution)/shard_map/ppermute | solution.py:94
  14.5 0.0 collective-permute-done.3
  14.5 0.0 collective-permute-start.10
  14.6 0.0 collective-permute-done.l2
  14.6 0.5 %collective-permute-start.4 = (f32[64,256]{1,0:T(8,128)S(1)}, f32[64,256]{1,0:T(8,128)S(1)}, u32[]{:S(2)}, u32[]{:S(2)}) collective-permute-start(f32[64,256]{1,0:T(8,128)S(1)} %bitcast.3), channel_id=1, source_target_pairs={{0,1},{1,0},{2,3},{3,2},{4,5},{5,4},{6,7},{7,6},{8,9},{9,8},{10,11... | collective-permute-start | bytes 196616 | tf_op jit(solution)/shard_map/ppermute | solution.py:94
  15.1 0.1 collective-permute-start.5
  15.2 0.0 collective-permute-done.8
  15.2 0.4 %collective-permute-start.9 = (f16[256,256]{1,0:T(8,128)(2,1)S(1)}, f16[256,256]{1,0:T(8,128)(2,1)S(1)}, u32[]{:S(2)}, u32[]{:S(2)}) collective-permute-start(f16[256,256]{1,0:T(8,128)(2,1)S(1)} %collective-permute-done.8), channel_id=1, source_target_pairs={{0,1},{1,0},{2,3},{3,2},{4,5},{5,4},{6,7},{7,6},{8,9},{9,8},{10,11... | collective-permute-start | bytes 393224 | tf_op jit(solution)/shard_map/ppermute | solution.py:94
  15.6 0.8 %collective-permute-done.6 = f16[256,256]{1,0:T(8,128)(2,1)S(1)} collective-permute-done((f16[256,256]{1,0:T(8,128)(2,1)S(1)}, f16[256,256]{1,0:T(8,128)(2,1)S(1)}, u32[]{:S(2)}, u32[]{:S(2)}) %collective-permute-start.6) | collective-permute-done | bytes 131104 | tf_op jit(solution)/shard_map/ppermute | solution.py:94
  16.4 0.0 collective-permute-start.7
  16.4 0.0 collective-permute-done.4.l1
  16.4 0.0 collective-permute-done.5.l3
  16.4 0.6 %shard_map.37 = (bf16[4,256,256]{2,1,0:T(8,128)(2,1)S(1)}, bf16[256,256]{1,0:T(8,128)(2,1)S(1)}, bf16[256,256]{1,0:T(8,128)(2,1)S(1)}) custom-call(s32[1]{0:T(128)} %bitcast.c_ref, bf16[2048,512]{1,0:T(8,128)(2,1)S(1)} %copy-done, f32[64,256]{1,0:T(8,128)S(1)} %bitcast.4, f32[64,256]{1,0:T(8,128)S(1)} %collective-permute-done.4.l1, ...), custom_call_target="tpu_custom_call" | custom-call | tf_op jit(solution)/shard_map/pallas_call | solution.py:131
  17.1 0.0 collective-permute-done.9
  17.1 0.4 %shard_map.39.sc = bf16[2,256,256]{2,1,0:T(8,128)(2,1)S(1)} custom-call(bf16[256,256]{1,0:T(8,128)(2,1)S(1)} %get-tuple-element.21.hi_ref, bf16[256,256]{1,0:T(8,128)(2,1)S(1)} %get-tuple-element.22.lo_ref, f32[256,256]{1,0:T(8,128)S(1)} %convert_multiply_fusion.3.refs_0_, f32[256,256]{1,0:T(8,128)S(1)} %convert_multiply_fusion.2.refs_1_), custom_call_target="tpu_custom_call" | custom-call | tf_op jit(solution)/shard_map/pallas_call | solution.py:153
  17.5 0.2 %collective-permute-done.7 = f16[256,256]{1,0:T(8,128)(2,1)S(1)} collective-permute-done((f16[256,256]{1,0:T(8,128)(2,1)S(1)}, f16[256,256]{1,0:T(8,128)(2,1)S(1)}, u32[]{:S(2)}, u32[]{:S(2)}) %collective-permute-start.7) | collective-permute-done | bytes 131104 | tf_op jit(solution)/shard_map/ppermute | solution.py:94
  17.8 0.4 %shard_map.38.sb = bf16[2,256,256]{2,1,0:T(8,128)(2,1)S(1)} custom-call(bf16[256,256]{1,0:T(8,128)(2,1)S(1)} %get-tuple-element.21.hi_ref, bf16[256,256]{1,0:T(8,128)(2,1)S(1)} %get-tuple-element.22.lo_ref, f32[256,256]{1,0:T(8,128)S(1)} %convert_multiply_fusion.5.refs_0_, f32[256,256]{1,0:T(8,128)S(1)} %convert_multiply_fusion.4.refs_1_), custom_call_target="tpu_custom_call" | custom-call | tf_op jit(solution)/shard_map/pallas_call | solution.py:153
  18.1 0.3 %collective-permute-done.10 = f16[512,256]{1,0:T(8,128)(2,1)S(1)} collective-permute-done((f16[512,256]{1,0:T(8,128)(2,1)S(1)}, f16[512,256]{1,0:T(8,128)(2,1)S(1)}, u32[]{:S(2)}, u32[]{:S(2)}) %collective-permute-start.10) | collective-permute-done | bytes 262176 | tf_op jit(solution)/shard_map/ppermute | solution.py:94
  18.5 0.1 convert_multiply_fusion
  18.5 2.0 %shard_map.40 = bf16[2048,512]{1,0:T(8,128)(2,1)} custom-call(s32[1]{0:T(128)} %bitcast.c_ref, bf16[2048,512]{1,0:T(8,128)(2,1)S(1)} %copy-done, bf16[4,256,256]{2,1,0:T(8,128)(2,1)S(1)} %get-tuple-element.20.sa, bf16[2,256,256]{2,1,0:T(8,128)(2,1)S(1)} %shard_map.38.sb, bf16[2,256,256]{2,1,0:T(8,128)(2,1)S(1)} %shard_map.39.sc, ...), custom_call_target="tpu_custom_call" | custom-call | tf_op jit(solution)/shard_map/pallas_call | solution.py:187
  (10 shorter events, 0.2 us)
Async XLA Ops:
  0.0 4.1 %collective-permute-start.1 = (f32[512,256]{1,0:T(8,128)}, f32[512,256]{1,0:T(8,128)S(1)}, u32[]{:S(2)}, u32[]{:S(2)}) collective-permute-start(f32[512,256]{1,0:T(8,128)} %param.4), channel_id=1, source_target_pairs={{0,1},{1,0},{2,3},{3,2},{4,5},{5,4},{6,7},{7,6},{8,9},{9,8},{10,11... | collective-permute-start | bytes 1572872 | tf_op jit(solution)/shard_map/ppermute | solution.py:94
  0.5 14.1 %collective-permute-start = (f32[64,256]{1,0:T(8,128)}, f32[64,256]{1,0:T(8,128)S(1)}, u32[]{:S(2)}, u32[]{:S(2)}) collective-permute-start(f32[64,256]{1,0:T(8,128)} %bitcast.2), channel_id=1, source_target_pairs={{0,2},{1,3},{2,0},{3,1},{4,6},{5,7},{6,4},{7,5},{8,10},{9,11},{10,... | collective-permute-start | bytes 196616 | tf_op jit(solution)/shard_map/ppermute | solution.py:94
  4.1 10.5 %copy-start.1 = (f32[256,64]{0,1:T(8,128)S(1)}, f32[256,64]{0,1:T(8,128)}, u32[]{:S(2)}) copy-start(f32[256,64]{0,1:T(8,128)} %param.5) | copy-start | bytes 196612
  4.2 12.3 %copy-start = (bf16[2048,512]{1,0:T(8,128)(2,1)S(1)}, bf16[2048,512]{1,0:T(8,128)(2,1)}, u32[]{:S(2)}) copy-start(bf16[2048,512]{1,0:T(8,128)(2,1)} %t_ref.1) | copy-start | bytes 6291460
  4.2 10.3 %collective-permute-start.3 = (f16[256,256]{1,0:T(8,128)(2,1)S(1)}, f16[256,256]{1,0:T(8,128)(2,1)S(1)}, u32[]{:S(2)}, u32[]{:S(2)}) collective-permute-start(f16[256,256]{1,0:T(8,128)(2,1)S(1)} %slice_select_fusion), channel_id=1, source_target_pairs={{0,24},{1,0},{2,3},{3,1},{5,29},{4,5},{7,6},{6,4},{8,18},{9,10},{1... | collective-permute-start | bytes 393224 | tf_op jit(solution)/shard_map/ppermute | solution.py:94
  7.9 6.6 %collective-permute-start.2 = (f16[256,256]{1,0:T(8,128)(2,1)S(1)}, f16[256,256]{1,0:T(8,128)(2,1)S(1)}, u32[]{:S(2)}, u32[]{:S(2)}) collective-permute-start(f16[256,256]{1,0:T(8,128)(2,1)S(1)} %slice_select_fusion), channel_id=1, source_target_pairs={{0,8},{1,16},{2,3},{3,1},{5,13},{4,21},{7,6},{6,4},{8,2},{9,26},{1... | collective-permute-start | bytes 393224 | tf_op jit(solution)/shard_map/ppermute | solution.py:94
  7.9 7.2 %collective-permute-start.8 = (f16[256,256]{1,0:T(8,128)(2,1)S(1)}, f16[256,256]{1,0:T(8,128)(2,1)S(1)}, u32[]{:S(2)}, u32[]{:S(2)}) collective-permute-start(f16[256,256]{1,0:T(8,128)(2,1)S(1)} %get-tuple-element.27), channel_id=1, source_target_pairs={{0,2},{1,3},{2,0},{3,1},{4,6},{5,7},{6,4},{7,5},{8,10},{9,11},{10,... | collective-permute-start | bytes 393224 | tf_op jit(solution)/shard_map/ppermute | solution.py:94
  8.0 8.4 %collective-permute-start.6 = (f16[256,256]{1,0:T(8,128)(2,1)S(1)}, f16[256,256]{1,0:T(8,128)(2,1)S(1)}, u32[]{:S(2)}, u32[]{:S(2)}) collective-permute-start(f16[256,256]{1,0:T(8,128)(2,1)S(1)} %get-tuple-element.28), channel_id=1, source_target_pairs={{0,2},{1,3},{2,0},{3,1},{4,6},{5,7},{6,4},{7,5},{8,10},{9,11},{10,... | collective-permute-start | bytes 393224 | tf_op jit(solution)/shard_map/ppermute | solution.py:94
  14.5 3.9 %collective-permute-start.10 = (f16[512,256]{1,0:T(8,128)(2,1)S(1)}, f16[512,256]{1,0:T(8,128)(2,1)S(1)}, u32[]{:S(2)}, u32[]{:S(2)}) collective-permute-start(f16[512,256]{1,0:T(8,128)(2,1)S(1)} %constant_dynamic-update-slice_fusion), channel_id=1, source_target_pairs={{0,4},{1,0},{2,6},{3,2},{4,5},{5,1},{6,7},{7,3},{8,12},{9,8},{10,1... | collective-permute-start | bytes 786440 | tf_op jit(solution)/shard_map/ppermute | solution.py:94
  14.6 1.8 %collective-permute-start.4 = (f32[64,256]{1,0:T(8,128)S(1)}, f32[64,256]{1,0:T(8,128)S(1)}, u32[]{:S(2)}, u32[]{:S(2)}) collective-permute-start(f32[64,256]{1,0:T(8,128)S(1)} %bitcast.3), channel_id=1, source_target_pairs={{0,1},{1,0},{2,3},{3,2},{4,5},{5,4},{6,7},{7,6},{8,9},{9,8},{10,11... | collective-permute-start | bytes 196616 | tf_op jit(solution)/shard_map/ppermute | solution.py:94
  15.1 1.3 %collective-permute-start.5 = (f32[64,256]{1,0:T(8,128)S(1)}, f32[64,256]{1,0:T(8,128)S(1)}, u32[]{:S(2)}, u32[]{:S(2)}) collective-permute-start(f32[64,256]{1,0:T(8,128)S(1)} %collective-permute-done.l2), channel_id=1, source_target_pairs={{0,1},{1,0},{2,3},{3,2},{4,5},{5,4},{6,7},{7,6},{8,9},{9,8},{10,11... | collective-permute-start | bytes 196616 | tf_op jit(solution)/shard_map/ppermute | solution.py:94
  15.2 1.9 %collective-permute-start.9 = (f16[256,256]{1,0:T(8,128)(2,1)S(1)}, f16[256,256]{1,0:T(8,128)(2,1)S(1)}, u32[]{:S(2)}, u32[]{:S(2)}) collective-permute-start(f16[256,256]{1,0:T(8,128)(2,1)S(1)} %collective-permute-done.8), channel_id=1, source_target_pairs={{0,1},{1,0},{2,3},{3,2},{4,5},{5,4},{6,7},{7,6},{8,9},{9,8},{10,11... | collective-permute-start | bytes 393224 | tf_op jit(solution)/shard_map/ppermute | solution.py:94
  16.4 1.3 %collective-permute-start.7 = (f16[256,256]{1,0:T(8,128)(2,1)S(1)}, f16[256,256]{1,0:T(8,128)(2,1)S(1)}, u32[]{:S(2)}, u32[]{:S(2)}) collective-permute-start(f16[256,256]{1,0:T(8,128)(2,1)S(1)} %collective-permute-done.6), channel_id=1, source_target_pairs={{0,1},{1,0},{2,3},{3,2},{4,5},{5,4},{6,7},{7,6},{8,9},{9,8},{10,11... | collective-permute-start | bytes 393224 | tf_op jit(solution)/shard_map/ppermute | solution.py:94

commit v8 on v6

--- a/solution.py
+++ b/solution.py
@@ -72,9 +72,10 @@
     pairs = []
     for z in range(4):
         for x in range(2):
-            pairs.append((dev(z, x, 0, x), dev(z ^ 3, x, z % 2, x)))
+            far = 1 if z % 2 else x
+            pairs.append((dev(z, x, 0, far), dev(z ^ 3, x, z % 2, x)))
             if z % 2:
-                pairs.append((dev(z, x, 0, 1 - x), dev(z, x, 1, x)))
+                pairs.append((dev(z, x, 0, 1 - far), dev(z, x, 1, x)))
                 pairs.append((dev(z, x, 1, x), dev(z, x, 1, 1 - x)))
                 pairs.append((dev(z, x, 1, 1 - x), dev(z, x, 0, 1 - x)))
             else:

time: 20.7 us -> 20.7 us (level)
  transfers between devices with their start and end apart: 11 -> 11, of which waited for: 4 -> 6; matrix products, arithmetic and copies ran while one was open for 7% -> 7% of each run, Pallas kernels for 6% -> 6%
where the time goes in v8:
time: 20.7 us; the launch traced here: 20.5 us
  starting transfers between devices  9.75 us (47%)
  waiting for transfers between devices  5.86 us (28%)
  Pallas kernels  3.15 us (15%)
  other arithmetic  1.48 us (7%)
    ppermute x11, starting transfers between devices, send(): return lax.ppermute(value, AXES, pairs)  9.75 us
    ppermute x11, waiting for transfers between devices, send(): return lax.ppermute(value, AXES, pairs)  5.86 us
    pallas_call x1, Pallas kernels, final(): pl.pallas_call(final_kernel, out_shape=jax.ShapeDtypeStruct((rows, cols),...  1.97 us
    convert_element_type x2, other arithmetic, narrow(): return (value * SCALE).astype(F16)  1.15 us
    pallas_call x1, Pallas kernels, early(): pl.pallas_call(early_kernel, out_shape=(jax.ShapeDtypeStruct((len(parts),...  0.61 us
    pallas_call x1, Pallas kernels, late(): pl.pallas_call(late_kernel, out_shape=jax.ShapeDtypeStruct((len(parts), n...  0.58 us
  transfers between devices with their start and end apart: 11, of which 6 were waited for; matrix products, arithmetic and copies ran while one was open for 7% of the time, Pallas kernels for 6%

profile of v8, /device:TPU:0, one launch (start us, length us, event | category | flops | bytes accessed | tf_op | source)
XLA Modules:
  0.0 20.5 jit_solution(10496880126805224386)
XLA Ops:
  0.0 0.5 %collective-permute-start.1 = (f32[512,256]{1,0:T(8,128)}, f32[512,256]{1,0:T(8,128)S(1)}, u32[]{:S(2)}, u32[]{:S(2)}) collective-permute-start(f32[512,256]{1,0:T(8,128)} %param.4), channel_id=1, source_target_pairs={{0,1},{1,0},{2,3},{3,2},{4,5},{5,4},{6,7},{7,6},{8,9},{9,8},{10,11... | collective-permute-start | bytes 1572872 | tf_op jit(solution)/shard_map/ppermute | solution.py:95
  0.5 2.5 %collective-permute-start = (f32[64,256]{1,0:T(8,128)}, f32[64,256]{1,0:T(8,128)S(1)}, u32[]{:S(2)}, u32[]{:S(2)}) collective-permute-start(f32[64,256]{1,0:T(8,128)} %bitcast.2), channel_id=1, source_target_pairs={{0,2},{1,3},{2,0},{3,1},{4,6},{5,7},{6,4},{7,5},{8,10},{9,11},{10,... | collective-permute-start | bytes 196616 | tf_op jit(solution)/shard_map/ppermute | solution.py:95
  3.0 1.1 %multiply_convert_fusion.1 = f16[512,256]{1,0:T(8,128)(2,1)S(1)} fusion(f32[512,256]{1,0:T(8,128)} %param.4), kind=kLoop, calls=%fused_computation.1 | loop fusion | flops 262144 | bytes 786432 | tf_op jit(solution)/shard_map/convert_element_type | solution.py:207
  4.1 0.0 copy-start.1
  4.1 0.0 collective-permute-done.1
  4.1 0.1 multiply_convert_fusion
  4.2 0.0 copy-start
  4.2 3.7 %collective-permute-start.3 = (f16[256,256]{1,0:T(8,128)(2,1)S(1)}, f16[256,256]{1,0:T(8,128)(2,1)S(1)}, u32[]{:S(2)}, u32[]{:S(2)}) collective-permute-start(f16[256,256]{1,0:T(8,128)(2,1)S(1)} %slice_select_fusion), channel_id=1, source_target_pairs={{0,24},{1,0},{2,3},{3,1},{5,29},{4,5},{7,6},{6,4},{9,18},{8,10},{1... | collective-permute-start | bytes 393224 | tf_op jit(solution)/shard_map/ppermute | solution.py:95
  7.9 0.0 collective-permute-start.2
  7.9 0.1 collective-permute-start.7
  8.0 2.0 %collective-permute-start.6 = (f16[256,256]{1,0:T(8,128)(2,1)S(1)}, f16[256,256]{1,0:T(8,128)(2,1)S(1)}, u32[]{:S(2)}, u32[]{:S(2)}) collective-permute-start(f16[256,256]{1,0:T(8,128)(2,1)S(1)} %get-tuple-element.28), channel_id=1, source_target_pairs={{0,2},{1,3},{2,0},{3,1},{4,6},{5,7},{6,4},{7,5},{8,10},{9,11},{10,... | collective-permute-start | bytes 393224 | tf_op jit(solution)/shard_map/ppermute | solution.py:95
  10.0 0.1 convert_multiply_fusion.6
  10.1 4.3 %collective-permute-done.2 = f16[256,256]{1,0:T(8,128)(2,1)S(1)} collective-permute-done((f16[256,256]{1,0:T(8,128)(2,1)S(1)}, f16[256,256]{1,0:T(8,128)(2,1)S(1)}, u32[]{:S(2)}, u32[]{:S(2)}) %collective-permute-start.2) | collective-permute-done | bytes 131104 | tf_op jit(solution)/shard_map/ppermute | solution.py:95
  14.5 0.0 collective-permute-done.3
  14.5 0.0 collective-permute-start.10
  14.6 0.0 collective-permute-done.l2
  14.6 0.5 %collective-permute-start.4 = (f32[64,256]{1,0:T(8,128)S(1)}, f32[64,256]{1,0:T(8,128)S(1)}, u32[]{:S(2)}, u32[]{:S(2)}) collective-permute-start(f32[64,256]{1,0:T(8,128)S(1)} %bitcast.3), channel_id=1, source_target_pairs={{0,1},{1,0},{2,3},{3,2},{4,5},{5,4},{6,7},{7,6},{8,9},{9,8},{10,11... | collective-permute-start | bytes 196616 | tf_op jit(solution)/shard_map/ppermute | solution.py:95
  15.1 0.1 collective-permute-start.5
  15.2 0.0 collective-permute-done.7
  15.2 0.4 %collective-permute-start.9 = (f16[256,256]{1,0:T(8,128)(2,1)S(1)}, f16[256,256]{1,0:T(8,128)(2,1)S(1)}, u32[]{:S(2)}, u32[]{:S(2)}) collective-permute-start(f16[256,256]{1,0:T(8,128)(2,1)S(1)} %collective-permute-done.7), channel_id=1, source_target_pairs={{0,1},{1,0},{2,3},{3,2},{4,5},{5,4},{6,7},{7,6},{8,9},{9,8},{10,11... | collective-permute-start | bytes 393224 | tf_op jit(solution)/shard_map/ppermute | solution.py:95
  15.6 0.2 collective-permute-done.6
  15.8 0.0 collective-permute-start.8
  15.9 0.3 %collective-permute-done.4.l1 = f32[64,256]{1,0:T(8,128)S(1)} collective-permute-done((f32[64,256]{1,0:T(8,128)S(1)}, f32[64,256]{1,0:T(8,128)S(1)}, u32[]{:S(2)}, u32[]{:S(2)}) %collective-permute-start.4) | collective-permute-done | bytes 65568 | tf_op jit(solution)/shard_map/ppermute | solution.py:95
  16.2 0.1 collective-permute-done.5.l3
  16.3 0.0 copy-done
  16.3 0.6 %shard_map.37 = (bf16[4,256,256]{2,1,0:T(8,128)(2,1)S(1)}, bf16[256,256]{1,0:T(8,128)(2,1)S(1)}, bf16[256,256]{1,0:T(8,128)(2,1)S(1)}) custom-call(s32[1]{0:T(128)} %bitcast.c_ref, bf16[2048,512]{1,0:T(8,128)(2,1)S(1)} %copy-done, f32[64,256]{1,0:T(8,128)S(1)} %bitcast.4, f32[64,256]{1,0:T(8,128)S(1)} %collective-permute-done.4.l1, ...), custom_call_target="tpu_custom_call" | custom-call | tf_op jit(solution)/shard_map/pallas_call | solution.py:132
  17.0 0.0 collective-permute-done.9
  17.0 0.2 collective-permute-done.8
  17.2 0.6 %shard_map.38.sb = bf16[4,256,256]{2,1,0:T(8,128)(2,1)S(1)} custom-call(bf16[256,256]{1,0:T(8,128)(2,1)S(1)} %get-tuple-element.21.hi_ref, bf16[256,256]{1,0:T(8,128)(2,1)S(1)} %get-tuple-element.22.lo_ref, f32[256,256]{1,0:T(8,128)S(1)} %convert_multiply_fusion.5.refs_0_, f32[256,256]{1,0:T(8,128)S(1)} %convert_multiply_fusion.4.refs_1_, ...), custom_call_target="tpu_custom_call" | custom-call | tf_op jit(solution)/shard_map/pallas_call | solution.py:154
  17.8 0.7 %collective-permute-done.10 = f16[512,256]{1,0:T(8,128)(2,1)S(1)} collective-permute-done((f16[512,256]{1,0:T(8,128)(2,1)S(1)}, f16[512,256]{1,0:T(8,128)(2,1)S(1)}, u32[]{:S(2)}, u32[]{:S(2)}) %collective-permute-start.10) | collective-permute-done | bytes 262176 | tf_op jit(solution)/shard_map/ppermute | solution.py:95
  18.5 0.1 convert_multiply_fusion
  18.5 2.0 %shard_map.39 = bf16[2048,512]{1,0:T(8,128)(2,1)} custom-call(s32[1]{0:T(128)} %bitcast.c_ref, bf16[2048,512]{1,0:T(8,128)(2,1)S(1)} %copy-done, bf16[4,256,256]{2,1,0:T(8,128)(2,1)S(1)} %get-tuple-element.20.sa, bf16[4,256,256]{2,1,0:T(8,128)(2,1)S(1)} %shard_map.38.sb, f32[256,256]{1,0:T(8,128)S(1)} %get-tuple-element.26.ta, ...), custom_call_target="tpu_custom_call" | custom-call | tf_op jit(solution)/shard_map/pallas_call | solution.py:188
  (9 shorter events, 0.2 us)
Async XLA Ops:
  0.0 4.1 %collective-permute-start.1 = (f32[512,256]{1,0:T(8,128)}, f32[512,256]{1,0:T(8,128)S(1)}, u32[]{:S(2)}, u32[]{:S(2)}) collective-permute-start(f32[512,256]{1,0:T(8,128)} %param.4), channel_id=1, source_target_pairs={{0,1},{1,0},{2,3},{3,2},{4,5},{5,4},{6,7},{7,6},{8,9},{9,8},{10,11... | collective-permute-start | bytes 1572872 | tf_op jit(solution)/shard_map/ppermute | solution.py:95
  0.5 14.1 %collective-permute-start = (f32[64,256]{1,0:T(8,128)}, f32[64,256]{1,0:T(8,128)S(1)}, u32[]{:S(2)}, u32[]{:S(2)}) collective-permute-start(f32[64,256]{1,0:T(8,128)} %bitcast.2), channel_id=1, source_target_pairs={{0,2},{1,3},{2,0},{3,1},{4,6},{5,7},{6,4},{7,5},{8,10},{9,11},{10,... | collective-permute-start | bytes 196616 | tf_op jit(solution)/shard_map/ppermute | solution.py:95
  4.1 10.5 %copy-start.1 = (f32[256,64]{0,1:T(8,128)S(1)}, f32[256,64]{0,1:T(8,128)}, u32[]{:S(2)}) copy-start(f32[256,64]{0,1:T(8,128)} %param.5) | copy-start | bytes 196612
  4.2 12.2 %copy-start = (bf16[2048,512]{1,0:T(8,128)(2,1)S(1)}, bf16[2048,512]{1,0:T(8,128)(2,1)}, u32[]{:S(2)}) copy-start(bf16[2048,512]{1,0:T(8,128)(2,1)} %t_ref.1) | copy-start | bytes 6291460
  4.2 10.3 %collective-permute-start.3 = (f16[256,256]{1,0:T(8,128)(2,1)S(1)}, f16[256,256]{1,0:T(8,128)(2,1)S(1)}, u32[]{:S(2)}, u32[]{:S(2)}) collective-permute-start(f16[256,256]{1,0:T(8,128)(2,1)S(1)} %slice_select_fusion), channel_id=1, source_target_pairs={{0,24},{1,0},{2,3},{3,1},{5,29},{4,5},{7,6},{6,4},{9,18},{8,10},{1... | collective-permute-start | bytes 393224 | tf_op jit(solution)/shard_map/ppermute | solution.py:95
  7.9 6.6 %collective-permute-start.2 = (f16[256,256]{1,0:T(8,128)(2,1)S(1)}, f16[256,256]{1,0:T(8,128)(2,1)S(1)}, u32[]{:S(2)}, u32[]{:S(2)}) collective-permute-start(f16[256,256]{1,0:T(8,128)(2,1)S(1)} %slice_select_fusion), channel_id=1, source_target_pairs={{0,8},{1,16},{2,3},{3,1},{5,13},{4,21},{7,6},{6,4},{8,2},{9,26},{1... | collective-permute-start | bytes 393224 | tf_op jit(solution)/shard_map/ppermute | solution.py:95
  7.9 7.2 %collective-permute-start.7 = (f16[256,256]{1,0:T(8,128)(2,1)S(1)}, f16[256,256]{1,0:T(8,128)(2,1)S(1)}, u32[]{:S(2)}, u32[]{:S(2)}) collective-permute-start(f16[256,256]{1,0:T(8,128)(2,1)S(1)} %get-tuple-element.27), channel_id=1, source_target_pairs={{0,2},{1,3},{2,0},{3,1},{4,6},{5,7},{6,4},{7,5},{8,10},{9,11},{10,... | collective-permute-start | bytes 393224 | tf_op jit(solution)/shard_map/ppermute | solution.py:95
  8.0 7.8 %collective-permute-start.6 = (f16[256,256]{1,0:T(8,128)(2,1)S(1)}, f16[256,256]{1,0:T(8,128)(2,1)S(1)}, u32[]{:S(2)}, u32[]{:S(2)}) collective-permute-start(f16[256,256]{1,0:T(8,128)(2,1)S(1)} %get-tuple-element.28), channel_id=1, source_target_pairs={{0,2},{1,3},{2,0},{3,1},{4,6},{5,7},{6,4},{7,5},{8,10},{9,11},{10,... | collective-permute-start | bytes 393224 | tf_op jit(solution)/shard_map/ppermute | solution.py:95
  14.5 3.9 %collective-permute-start.10 = (f16[512,256]{1,0:T(8,128)(2,1)S(1)}, f16[512,256]{1,0:T(8,128)(2,1)S(1)}, u32[]{:S(2)}, u32[]{:S(2)}) collective-permute-start(f16[512,256]{1,0:T(8,128)(2,1)S(1)} %constant_dynamic-update-slice_fusion), channel_id=1, source_target_pairs={{0,4},{1,0},{2,6},{3,2},{4,5},{5,1},{6,7},{7,3},{8,12},{9,8},{10,1... | collective-permute-start | bytes 786440 | tf_op jit(solution)/shard_map/ppermute | solution.py:95
  14.6 1.6 %collective-permute-start.4 = (f32[64,256]{1,0:T(8,128)S(1)}, f32[64,256]{1,0:T(8,128)S(1)}, u32[]{:S(2)}, u32[]{:S(2)}) collective-permute-start(f32[64,256]{1,0:T(8,128)S(1)} %bitcast.3), channel_id=1, source_target_pairs={{0,1},{1,0},{2,3},{3,2},{4,5},{5,4},{6,7},{7,6},{8,9},{9,8},{10,11... | collective-permute-start | bytes 196616 | tf_op jit(solution)/shard_map/ppermute | solution.py:95
  15.1 1.3 %collective-permute-start.5 = (f32[64,256]{1,0:T(8,128)S(1)}, f32[64,256]{1,0:T(8,128)S(1)}, u32[]{:S(2)}, u32[]{:S(2)}) collective-permute-start(f32[64,256]{1,0:T(8,128)S(1)} %collective-permute-done.l2), channel_id=1, source_target_pairs={{0,1},{1,0},{2,3},{3,2},{4,5},{5,4},{6,7},{7,6},{8,9},{9,8},{10,11... | collective-permute-start | bytes 196616 | tf_op jit(solution)/shard_map/ppermute | solution.py:95
  15.2 1.8 %collective-permute-start.9 = (f16[256,256]{1,0:T(8,128)(2,1)S(1)}, f16[256,256]{1,0:T(8,128)(2,1)S(1)}, u32[]{:S(2)}, u32[]{:S(2)}) collective-permute-start(f16[256,256]{1,0:T(8,128)(2,1)S(1)} %collective-permute-done.7), channel_id=1, source_target_pairs={{0,1},{1,0},{2,3},{3,2},{4,5},{5,4},{6,7},{7,6},{8,9},{9,8},{10,11... | collective-permute-start | bytes 393224 | tf_op jit(solution)/shard_map/ppermute | solution.py:95
  15.8 1.3 %collective-permute-start.8 = (f16[256,256]{1,0:T(8,128)(2,1)S(1)}, f16[256,256]{1,0:T(8,128)(2,1)S(1)}, u32[]{:S(2)}, u32[]{:S(2)}) collective-permute-start(f16[256,256]{1,0:T(8,128)(2,1)S(1)} %collective-permute-done.6), channel_id=1, source_target_pairs={{0,1},{1,0},{2,3},{3,2},{4,5},{5,4},{6,7},{7,6},{8,9},{9,8},{10,11... | collective-permute-start | bytes 393224 | tf_op jit(solution)/shard_map/ppermute | solution.py:95
